TPU v7x, 32 devices: a whole 2x2x4 slice. The times are simulated.
32 devices in a mesh: grp: 2 (over y), ep: 4 (over z), tp: 2 (over x), sub: 2 (over core).
Axes of the slice: x: 2, y: 2, z: 4, core: 2. Of those that a mesh axis runs over, the one named last changes fastest.
Arguments:
- tokens: bfloat16 [1024, 4096], P(('grp', 'ep', 'sub'), 'tp'), parts along dimension 0, may hold values from -6 to 6
- expert_ids: int32 [1024, 2], P(('grp', 'ep', 'sub')), parts along dimension 0, may hold values from 0 to 7, all different within a row; in each aligned block of 64 rows (0 to 63, 64 to 127, ...) at most 48 rows name the same one
- gate_values: bfloat16 [1024, 2], P(('grp', 'ep', 'sub')), parts along dimension 0, may hold values from 0.099609375 to 1
- w_gate: bfloat16 [8, 4096, 1536], P(('ep', 'sub'), None, 'tp'), may hold values from -0.09375 to 0.09375
- w_up: bfloat16 [8, 4096, 1536], P(('ep', 'sub'), None, 'tp'), may hold values from -0.09375 to 0.09375
- w_down: bfloat16 [8, 1536, 4096], P(('ep', 'sub'), 'tp'), may hold values from -0.15625 to 0.15625
Outputs:
- mixed: bfloat16 [1024, 4096], P(('grp', 'ep', 'sub'), 'tp'), parts along dimension 0
There are 2 independent parts, one for each index of `grp`. A program takes and returns all parts, laid end to end along the dimension named above; an argument that names none is the same for every part. Nothing has to cross between parts.
Inputs may be any that keep to these rules, and one draw needn't show every extreme that they name: `expert_ids`: within each aligned block of 64 rows no expert is named by more than 48 rows, a bound that some block reaches; a row names 2 different experts.
All inputs are finite; a program needn't handle non-finite values.
Results may differ from a plain program's by a relative error of at most 0.0058.
Values may be sent and summed in bfloat16 or wider, within the bound.
No kernel may reach another device: no remote copies, remote signals or barrier semaphores. Data moves between devices by JAX's collectives and lax.ppermute only.
A program may use at most 128 MiB of HBM per device.

v0:
```python
import jax
import jax.numpy as jnp
from jax import lax
from jax.sharding import PartitionSpec as P


def slot_positions(ids_block, experts, capacity):
    flat_ids = ids_block.reshape(-1)
    one_hot = (flat_ids[:, None] == jnp.arange(experts, dtype=jnp.int32)[None, :]).astype(jnp.int32)
    earlier = jnp.cumsum(one_hot, axis=0) - one_hot
    slot_idx = jnp.sum(earlier * one_hot, axis=1)
    return (flat_ids * capacity + slot_idx).reshape(ids_block.shape)


def on_device(tokens, expert_ids, gate_values, w_gate, w_up, w_down):
    peer_count = lax.axis_size(("ep", "sub"))
    tok_rows = tokens.shape[0]
    top_count = expert_ids.shape[1]
    capacity = 3 * tok_rows * top_count // peer_count
    lane_total = peer_count * capacity
    own_positions = slot_positions(expert_ids, peer_count, capacity)
    lane_ids = jnp.arange(lane_total, dtype=jnp.int32)
    lane_hits = own_positions[None, :, :] == lane_ids[:, None, None]
    dispatch_mat = jnp.any(lane_hits, axis=2).astype(jnp.bfloat16)
    weight_back = jnp.sum(
        jnp.where(lane_hits, gate_values.astype(jnp.float32)[None, :, :], jnp.float32(0.0)), axis=2
    )
    combine_mat = weight_back.T.astype(jnp.bfloat16)
    full_rows = lax.all_gather(tokens, "tp", axis=1, tiled=True)
    outgoing = jnp.dot(dispatch_mat, full_rows, preferred_element_type=jnp.float32).astype(
        jnp.bfloat16
    )
    outgoing = outgoing.reshape(peer_count, capacity, full_rows.shape[1])
    arrived = lax.all_to_all(outgoing, ("ep", "sub"), split_axis=0, concat_axis=0, tiled=True)
    flat_rows = arrived.reshape(peer_count * capacity, arrived.shape[2])
    gate_act = jnp.dot(flat_rows, w_gate[0], preferred_element_type=jnp.float32)
    up_act = jnp.dot(flat_rows, w_up[0], preferred_element_type=jnp.float32)
    hidden = (jax.nn.silu(gate_act) * up_act).astype(jnp.bfloat16)
    partial_value = jnp.dot(hidden, w_down[0], preferred_element_type=jnp.float32).astype(
        jnp.bfloat16
    )
    partial_value = partial_value.reshape(peer_count, capacity, w_down.shape[2])
    returned = lax.all_to_all(partial_value, ("ep", "sub"), split_axis=0, concat_axis=0, tiled=True)
    local_sum = jnp.dot(
        combine_mat,
        returned.reshape(lane_total, returned.shape[2]),
        preferred_element_type=jnp.float32,
    )
    mixed = lax.psum_scatter(local_sum, "tp", scatter_dimension=1, tiled=True)
    return mixed.astype(jnp.bfloat16)


def solution(mesh):
    in_specs = (
        P(("grp", "ep", "sub"), "tp"),
        P(("grp", "ep", "sub"), None),
        P(("grp", "ep", "sub"), None),
        P(("ep", "sub"), None, "tp"),
        P(("ep", "sub"), None, "tp"),
        P(("ep", "sub"), "tp", None),
    )
    out_specs = P(("grp", "ep", "sub"), "tp")
    return jax.shard_map(
        on_device, mesh=mesh, in_specs=in_specs, out_specs=out_specs, check_vma=False
    )
```

profile of v0, /device:TPU:0, one launch (start us, length us, event | category | flops | bytes accessed | tf_op | source)
XLA Modules:
  0.0 218.7 jit_solution(11064054089104735460)
XLA Ops:
  6.5 0.8 copy.19
  7.3 0.1 eq.28
  7.4 0.1 fusion.19
  7.5 0.2 reduce_window_sum.11
  7.7 0.2 select_reduce_fusion.1
  7.9 0.1 reduce_sum.21
  8.0 0.1 copy.20
  8.1 0.7 multiply_add_fusion
  8.8 0.1 fusion.18
  8.9 10.2 %all_gather.3 = bf16[64,4096]{1,0:T(8,128)(2,1)S(1)} all-gather(bf16[64,2048]{1,0:T(8,128)(2,1)} %param.6), channel_id=1, replica_groups=mesh['grp'=2,'ep'=4,'tp'=2,'sub'=2] {'tp'}, dimensions={1}, use_global_device_ids=true | all-gather | bytes 786432 | tf_op jit(solution)/shard_map/all_gather | solution.py:29
  19.1 1.0 convolution_convert_fusion
  20.1 0.0 copy-start
  20.1 76.7 %all_to_all.10 = bf16[8,48,4096]{2,1,0:T(8,128)(2,1)S(1)} all-to-all(bf16[8,48,4096]{2,1,0:T(8,128)(2,1)S(1)} %bitcast.28), channel_id=1, replica_groups=mesh['grp'=2,'ep'=4,'tp'=2,'sub'=2] {'ep','sub'}, dimensions={0} | all-to-all | bytes 6291456 | tf_op jit(solution)/shard_map/all_to_all | solution.py:34
  96.8 3.6 %fusion.4 = f32[384,768]{1,0:T(8,128)} fusion(bf16[384,4096]{1,0:T(8,128)(2,1)S(1)} %bitcast.30, bf16[1,4096,768]{2,1,0:T(8,128)(2,1)S(1)} %copy-done), kind=kOutput, calls=%fused_computation.4 | convolution fusion | flops 2415919104 | bytes 10616832 | tf_op jit(solution)/shard_map/dot_general | solution.py:36
  100.4 13.3 %fusion.6 = bf16[384,4096]{1,0:T(8,128)(2,1)} fusion(bf16[1,768,4096]{2,1,0:T(8,128)(2,1)} %param.11, bf16[384,4096]{1,0:T(8,128)(2,1)S(1)} %bitcast.31, bf16[1,4096,768]{2,1,0:T(8,128)(2,1)} %param.10, f32[384,768]{1,0:T(8,128)} %fusion.4), kind=kOutput, calls=%fused_computation.7 | convolution fusion | flops 4835180544 | bytes 20054016 | tf_op jit(solution)/shard_map/dot_general | solution.py:39
  113.8 3.8 %all-to-all-start.1 = ((bf16[8,48,4096]{2,1,0:T(8,128)(2,1)}), bf16[8,48,4096]{2,1,0:T(8,128)(2,1)S(1)}, u32[]{:S(2)}, u32[]{:S(2)}) async-start(bf16[8,48,4096]{2,1,0:T(8,128)(2,1)} %bitcast.29), calls=%async_computation.1 | async-start | bytes 6291456 | tf_op jit(solution)/shard_map/all_to_all | solution.py:43
  117.5 0.0 reduce-scatter.2.cloned.1.call-start
  117.6 0.0 copy-done.1
  117.6 0.1 select_reduce_fusion
  117.7 71.3 %all-to-all-done.1 = bf16[8,48,4096]{2,1,0:T(8,128)(2,1)S(1)} async-done(((bf16[8,48,4096]{2,1,0:T(8,128)(2,1)}), bf16[8,48,4096]{2,1,0:T(8,128)(2,1)S(1)}, u32[]{:S(2)}, u32[]{:S(2)}) %all-to-all-start.1) | async-done | bytes 3145760 | tf_op jit(solution)/shard_map/all_to_all | solution.py:43
  189.0 1.7 fusion.23
  190.7 0.0 reduce-scatter.2.cloned.1.call-update
  190.7 19.4 %reduce-scatter.2.cloned.1.call-done = f32[64,2048]{1,0:T(8,128)} async-done(((f32[64,4096]{1,0:T(8,128)}), f32[64,2048]{1,0:T(8,128)}) %reduce-scatter.2.cloned.1.call-update) | async-done | bytes 524304 | tf_op jit(solution)/shard_map/reduce_scatter | solution.py:49
  210.1 1.8 convert_element_type.29
  (3 shorter events, 0.0 us)
Async XLA Ops:
  20.1 76.7 %copy-start = (bf16[1,4096,768]{2,1,0:T(8,128)(2,1)S(1)}, bf16[1,4096,768]{2,1,0:T(8,128)(2,1)}, u32[]{:S(2)}) copy-start(bf16[1,4096,768]{2,1,0:T(8,128)(2,1)} %param.9) | copy-start | bytes 18874372
  113.8 3.8 %copy-start.1 = (bf16[64,2]{0,1:T(2,128)(2,1)S(1)}, bf16[64,2]{0,1:T(2,128)(2,1)}, u32[]{:S(2)}) copy-start(bf16[64,2]{0,1:T(2,128)(2,1)} %param.8) | copy-start | bytes 772
  113.8 75.2 %all-to-all-start.1 = ((bf16[8,48,4096]{2,1,0:T(8,128)(2,1)}), bf16[8,48,4096]{2,1,0:T(8,128)(2,1)S(1)}, u32[]{:S(2)}, u32[]{:S(2)}) async-start(bf16[8,48,4096]{2,1,0:T(8,128)(2,1)} %bitcast.29), calls=%async_computation.1 | async-start | bytes 6291456 | tf_op jit(solution)/shard_map/all_to_all | solution.py:43
  117.5 92.5 %reduce-scatter.2.cloned.1.call-start = ((), (), s32[]{:S(2)}) async-start(), calls=%async_computation.3 | async-start | bytes 1572864 | tf_op jit(solution)/shard_map/reduce_scatter | solution.py:49
Sparse Core Ops, SparseCore 0:
  190.8 19.1 reduce-scatter.1
where the time goes:
time: 219 us
  waiting for transfers between devices  90.6 us (41%)
  blocking collectives  86.9 us (40%)
  matrix products  19.7 us (9%)
  between operations  13.5 us (6%)
  starting transfers between devices  3.82 us (2%)
  other arithmetic  3.1 us (1%)
    all_to_all x1, blocking collectives, on_device(): lax.all_to_all(outgoing, ('ep', 'sub'), split_axis=0, concat_axis=0, tile...  76.7 us
    all_to_all x1, waiting for transfers between devices, on_device(): lax.all_to_all(partial_value, ('ep', 'sub'), split_axis=0, concat_axis=0,...  71.3 us
    reduce_scatter x1, waiting for transfers between devices, on_device(): mixed = lax.psum_scatter(local_sum, 'tp', scatter_dimension=1, tiled=True)  19.4 us
    dot_general x1, matrix products, on_device(): jnp.dot(hidden, w_down[0], preferred_element_type=jnp.float32)  13.3 us
    all_gather x1, blocking collectives, on_device(): full_rows = lax.all_gather(tokens, 'tp', axis=1, tiled=True)  10.2 us
  transfers between devices with their start and end apart: 2, of which 2 were waited for; matrix products, arithmetic and copies ran while one was open for 0% of the time, Pallas kernels for 0%

commit v1 on v0

--- a/solution.py
+++ b/solution.py
@@ -1,7 +1,13 @@
+import functools
+
 import jax
 import jax.numpy as jnp
 from jax import lax
+from jax.experimental import pallas as pl
+from jax.experimental.pallas import tpu as pltpu
 from jax.sharding import PartitionSpec as P
+
+LANES = 128
 
 
 def slot_positions(ids_block, experts, capacity):
@@ -12,7 +18,7 @@
     return (flat_ids * capacity + slot_idx).reshape(ids_block.shape)
 
 
-def on_device(tokens, expert_ids, gate_values, w_gate, w_up, w_down):
+def by_slots(tokens, expert_ids, gate_values, w_gate, w_up, w_down):
     peer_count = lax.axis_size(("ep", "sub"))
     tok_rows = tokens.shape[0]
     top_count = expert_ids.shape[1]
@@ -50,6 +56,96 @@
     return mixed.astype(jnp.bfloat16)
 
 
+def expert_kernel(where_ref, own_ref, other_ref, gate_ref, up_ref, down_ref, out_ref, hidden_ref, scale_ref):
+    half = gate_ref.shape[0] // 2
+    rows = own_ref.shape[1]
+    width = gate_ref.shape[1]
+    tp, expert = where_ref[0], where_ref[1]
+    mine = pl.ds(pl.multiple_of(tp * half, half), half)
+    peers = pl.ds(pl.multiple_of((1 - tp) * half, half), half)
+    sources = (own_ref, other_ref)
+    tile = 256 if width % 256 == 0 else width
+    lane = lax.broadcasted_iota(jnp.int32, (rows, LANES), 1)
+    for s, source in enumerate(sources):
+        weights = source[0, :, half:].astype(jnp.float32)
+        scale_ref[s] = jnp.sum(jnp.where(lane == expert, weights, 0.0), axis=1, keepdims=True)
+
+    @pl.loop(0, width // tile)
+    def _(j):
+        columns = pl.ds(pl.multiple_of(j * tile, tile), tile)
+        for s, source in enumerate(sources):
+            def act(weight_ref):
+                return jnp.dot(
+                    source[0, :, :half], weight_ref[mine, columns], preferred_element_type=jnp.float32
+                ) + jnp.dot(
+                    source[1, :, :half], weight_ref[peers, columns], preferred_element_type=jnp.float32
+                )
+            gate = act(gate_ref)
+            hidden_ref[s, :, columns] = (gate / (1.0 + jnp.exp(-gate)) * act(up_ref)).astype(jnp.bfloat16)
+
+    out_tile = 512
+    for h in range(2):
+        @pl.loop(0, half // out_tile)
+        def _(n):
+            to = pl.multiple_of(n * out_tile, out_tile)
+            start = pl.multiple_of((tp if h == 0 else 1 - tp) * half + n * out_tile, out_tile)
+            for s in range(2):
+                value = jnp.dot(
+                    hidden_ref[s], down_ref[:, pl.ds(start, out_tile)], preferred_element_type=jnp.float32
+                )
+                out_ref[s, h, :, pl.ds(to, out_tile)] = (value * scale_ref[s]).astype(jnp.bfloat16)
+
+
+def run_expert(where, own, other, w_gate, w_up, w_down):
+    rows, half = own.shape[1], w_gate.shape[0] // 2
+    width = w_gate.shape[1]
+    vmem = pl.BlockSpec(memory_space=pltpu.VMEM)
+    return pl.pallas_call(
+        expert_kernel,
+        out_shape=jax.ShapeDtypeStruct((2, 2, rows, half), jnp.bfloat16),
+        in_specs=[pl.BlockSpec(memory_space=pltpu.SMEM)] + [vmem] * 5,
+        out_specs=vmem,
+        scratch_shapes=[
+            pltpu.VMEM((2, rows, width), jnp.bfloat16),
+            pltpu.VMEM((2, rows, 1), jnp.float32),
+        ],
+        compiler_params=pltpu.CompilerParams(vmem_limit_bytes=48 * 1024 * 1024),
+        cost_estimate=pl.CostEstimate(
+            flops=2 * 2 * rows * 3 * 2 * half * width, bytes_accessed=3 * 2 * half * width * 2, transcendentals=0
+        ),
+    )(where, own, other, w_gate, w_up, w_down)
+
+
+def by_rows(tokens, expert_ids, gate_values, w_gate, w_up, w_down):
+    ep, sub = lax.axis_size("ep"), lax.axis_size("sub")
+    rows, half = tokens.shape
+    swap = [(0, 1), (1, 0)]
+    ahead = lambda k: [(i, (i + k) % ep) for i in range(ep)]
+    lanes = jnp.arange(LANES, dtype=jnp.int32)
+    weights = jnp.sum(
+        jnp.where(expert_ids[:, :, None] == lanes, gate_values.astype(jnp.float32)[:, :, None], 0.0), axis=1
+    )
+    packed = jnp.concatenate([tokens, weights.astype(jnp.bfloat16)], axis=1)
+    mine = [packed] + [lax.ppermute(packed, "ep", ahead(k)) for k in range(1, ep)]
+    peers = [lax.ppermute(a, "tp", swap) for a in mine]
+    own = jnp.stack(mine + peers).reshape(2, ep * rows, half + LANES)
+    other = lax.ppermute(own, "sub", swap)
+    where = jnp.stack([lax.axis_index("tp"), lax.axis_index("ep") * sub + lax.axis_index("sub")]).astype(jnp.int32)
+    out = run_expert(where, own, other, w_gate[0], w_up[0], w_down[0])
+    crossed = lax.ppermute(out[1], "sub", swap)
+    to_peer = out[0, 1].astype(jnp.float32) + crossed[1].astype(jnp.float32)
+    to_peer = to_peer.astype(jnp.bfloat16).reshape(ep, rows, half)
+    keep = out[0, 0].astype(jnp.float32) + crossed[0].astype(jnp.float32)
+    keep = keep.reshape(ep, rows, half)
+    total = None
+    for k in range(ep):
+        part = keep[k] + lax.ppermute(to_peer[k], "tp", swap).astype(jnp.float32)
+        if k:
+            part = lax.ppermute(part.astype(jnp.bfloat16), "ep", ahead(-k)).astype(jnp.float32)
+        total = part if total is None else total + part
+    return total.astype(jnp.bfloat16)
+
+
 def solution(mesh):
     in_specs = (
         P(("grp", "ep", "sub"), "tp"),
@@ -60,6 +156,7 @@
         P(("ep", "sub"), "tp", None),
     )
     out_specs = P(("grp", "ep", "sub"), "tp")
+    small = mesh.shape["tp"] == 2 and mesh.shape["sub"] == 2 and mesh.shape["ep"] <= 4
     return jax.shard_map(
-        on_device, mesh=mesh, in_specs=in_specs, out_specs=out_specs, check_vma=False
+        by_rows if small else by_slots, mesh=mesh, in_specs=in_specs, out_specs=out_specs, check_vma=False
     )

time: 219 us -> 121 us (0.55)
  blocking collectives: 86.9 us -> 0 us
  Pallas kernels: 0 us -> 21 us
  matrix products: 19.7 us -> 0 us
  waiting for transfers between devices: 90.6 us -> 74.1 us
  starting transfers between devices: 3.82 us -> 17.6 us
  between operations: 13.5 us -> 0.14 us
  other arithmetic: 3.1 us -> 5.33 us
    all_to_all x1 -> x0, blocking collectives: 76.7 us -> none  [on_device(): lax.all_to_all(outgoing, ('ep', 'sub'), split_axis=0, concat_axis=0, tile...]
    ppermute x0 -> x16, waiting for transfers between devices: none -> 74.1 us  [the longest x4 18.9 us: by_rows(): part = keep[k] + lax.ppermute(to_peer[k], 'tp', swap).astype(jnp.float32)]
    all_to_all x1 -> x0, waiting for transfers between devices: 71.3 us -> none  [on_device(): lax.all_to_all(partial_value, ('ep', 'sub'), split_axis=0, concat_axis=0,...]
    pallas_call x0 -> x1, Pallas kernels: none -> 21 us  [run_expert(): pl.pallas_call(expert_kernel, out_shape=jax.ShapeDtypeStruct((2, 2, rows,...]
    dot_general x4 -> x0, matrix products: 19.7 us -> none  [the longest x1 13.3 us: on_device(): jnp.dot(hidden, w_down[0], preferred_element_type=jnp.float32)]
    reduce_scatter x1 -> x0, waiting for transfers between devices: 19.4 us -> none  [on_device(): mixed = lax.psum_scatter(local_sum, 'tp', scatter_dimension=1, tiled=True)]
    ppermute x0 -> x16, starting transfers between devices: none -> 17.6 us  [the longest x3 6.11 us: by_rows(): lax.ppermute(packed, 'ep', ahead(k))]
    all_gather x1 -> x0, blocking collectives: 10.2 us -> none  [on_device(): full_rows = lax.all_gather(tokens, 'tp', axis=1, tiled=True)]
  transfers between devices with their start and end apart: 2 -> 16, of which waited for: 2 -> 12; matrix products, arithmetic and copies ran while one was open for 0% -> 1% of each run, Pallas kernels for 0% -> 0%
where the time goes in v1:
time: 121 us; the launch traced here: 120 us
  waiting for transfers between devices  74.1 us (61%)
  Pallas kernels  21 us (17%)
  starting transfers between devices  17.6 us (15%)
  other arithmetic  5.33 us (4%)
  local copies, waits for them, and re-layouts  2.15 us (2%)
    pallas_call x1, Pallas kernels, run_expert(): pl.pallas_call(expert_kernel, out_shape=jax.ShapeDtypeStruct((2, 2, rows,...  21 us
    ppermute x4, waiting for transfers between devices, by_rows(): part = keep[k] + lax.ppermute(to_peer[k], 'tp', swap).astype(jnp.float32)  18.9 us
    ppermute x3, waiting for transfers between devices, by_rows(): lax.ppermute(packed, 'ep', ahead(k))  18.7 us
    ppermute x3, waiting for transfers between devices, by_rows(): lax.ppermute(part.astype(jnp.bfloat16), 'ep', ahead(-k)).astype(jnp.float32)  16.8 us
    ppermute x4, waiting for transfers between devices, by_rows(): peers = [lax.ppermute(a, 'tp', swap) for a in mine]  11.3 us
    ppermute x3, starting transfers between devices, by_rows(): lax.ppermute(packed, 'ep', ahead(k))  6.11 us
    ppermute x4, starting transfers between devices, by_rows(): peers = [lax.ppermute(a, 'tp', swap) for a in mine]  5.01 us
    ppermute x1, waiting for transfers between devices, by_rows(): other = lax.ppermute(own, 'sub', swap)  4.38 us
  transfers between devices with their start and end apart: 16, of which 12 were waited for; matrix products, arithmetic and copies ran while one was open for 1% of the time, Pallas kernels for 0%

profile of v1, /device:TPU:0, one launch (start us, length us, event | category | flops | bytes accessed | tf_op | source)
XLA Modules:
  0.0 120.3 jit_solution(14864326867485253159)
XLA Ops:
  1.4 1.0 pad_maximum_fusion
  2.4 5.1 %collective-permute-start.2 = (bf16[64,2176]{1,0:T(8,128)(2,1)S(1)}, bf16[64,2176]{1,0:T(8,128)(2,1)S(1)}, u32[]{:S(2)}, u32[]{:S(2)}) collective-permute-start(bf16[64,2176]{1,0:T(8,128)(2,1)S(1)} %pad_maximum_fusion), channel_id=1, source_target_pairs={{0,12},{4,0},{8,4},{12,8},{1,13},{5,1},{9,5},{13,9},{2,14},{6,2},{... | collective-permute-start | bytes 835592 | tf_op jit(solution)/shard_map/ppermute | solution.py:129
  7.5 1.0 collective-permute-start
  8.5 1.5 %collective-permute-start.3 = (bf16[64,2176]{1,0:T(8,128)(2,1)S(1)}, bf16[64,2176]{1,0:T(8,128)(2,1)S(1)}, u32[]{:S(2)}, u32[]{:S(2)}) collective-permute-start(bf16[64,2176]{1,0:T(8,128)(2,1)S(1)} %pad_maximum_fusion), channel_id=1, source_target_pairs={{0,2},{2,0},{1,3},{3,1},{4,6},{6,4},{5,7},{7,5},{8,10},{10,8},{9,1... | collective-permute-start | bytes 835592 | tf_op jit(solution)/shard_map/ppermute | solution.py:130
  10.0 1.0 bitcast_dynamic-update-slice_fusion.7
  11.0 3.6 %collective-permute-done.2 = bf16[64,2176]{1,0:T(8,128)(2,1)S(1)} collective-permute-done((bf16[64,2176]{1,0:T(8,128)(2,1)S(1)}, bf16[64,2176]{1,0:T(8,128)(2,1)S(1)}, u32[]{:S(2)}, u32[]{:S(2)}) %collective-permute-start.2) | collective-permute-done | bytes 278560 | tf_op jit(solution)/shard_map/ppermute | solution.py:129
  14.6 1.5 %collective-permute-start.6 = (bf16[64,2176]{1,0:T(8,128)(2,1)S(1)}, bf16[64,2176]{1,0:T(8,128)(2,1)S(1)}, u32[]{:S(2)}, u32[]{:S(2)}) collective-permute-start(bf16[64,2176]{1,0:T(8,128)(2,1)S(1)} %collective-permute-done.2), channel_id=1, source_target_pairs={{0,2},{2,0},{1,3},{3,1},{4,6},{6,4},{5,7},{7,5},{8,10},{10,8},{9,1... | collective-permute-start | bytes 835592 | tf_op jit(solution)/shard_map/ppermute | solution.py:130
  16.1 15.1 %collective-permute-done.1 = bf16[64,2176]{1,0:T(8,128)(2,1)S(1)} collective-permute-done((bf16[64,2176]{1,0:T(8,128)(2,1)S(1)}, bf16[64,2176]{1,0:T(8,128)(2,1)S(1)}, u32[]{:S(2)}, u32[]{:S(2)}) %collective-permute-start.1) | collective-permute-done | bytes 278560 | tf_op jit(solution)/shard_map/ppermute | solution.py:129
  31.2 1.5 %collective-permute-start.5 = (bf16[64,2176]{1,0:T(8,128)(2,1)S(1)}, bf16[64,2176]{1,0:T(8,128)(2,1)S(1)}, u32[]{:S(2)}, u32[]{:S(2)}) collective-permute-start(bf16[64,2176]{1,0:T(8,128)(2,1)S(1)} %collective-permute-done.1), channel_id=1, source_target_pairs={{0,2},{2,0},{1,3},{3,1},{4,6},{6,4},{5,7},{7,5},{8,10},{10,8},{9,1... | collective-permute-start | bytes 835592 | tf_op jit(solution)/shard_map/ppermute | solution.py:130
  33.4 11.3 %collective-permute-done.4 = bf16[64,2176]{1,0:T(8,128)(2,1)S(1)} collective-permute-done((bf16[64,2176]{1,0:T(8,128)(2,1)S(1)}, bf16[64,2176]{1,0:T(8,128)(2,1)S(1)}, u32[]{:S(2)}, u32[]{:S(2)}) %collective-permute-start.4) | collective-permute-done | bytes 278560 | tf_op jit(solution)/shard_map/ppermute | solution.py:130
  45.0 4.4 %collective-permute-done.7.other_ref = bf16[2,256,2176]{2,1,0:T(8,128)(2,1)} collective-permute-done((bf16[2,256,2176]{2,1,0:T(8,128)(2,1)S(1)}, bf16[2,256,2176]{2,1,0:T(8,128)(2,1)}, u32[]{:S(2)}, u32[]{:S(2)}) %collective-permute-start.7) | collective-permute-done | bytes 2228256 | tf_op jit(solution)/shard_map/ppermute | solution.py:132
  49.4 21.0 %shard_map.64 = bf16[2,2,256,2048]{3,2,1,0:T(8,128)(2,1)} custom-call(s32[2]{0:T(128)S(1)} %pad_add_fusion.where_ref, bf16[2,256,2176]{2,1,0:T(8,128)(2,1)S(1)} %bitcast.45, bf16[2,256,2176]{2,1,0:T(8,128)(2,1)} %collective-permute-done.7.other_ref, bf16[4096,768]{1,0:T(8,128)(2,1)} %bitcast.46, bf16[4096,768]{1,0:T(8,128)(2,1)} %bitcast.47, ...), custom_call_target="tpu_custom_call" | custom-call | flops 9663676416 | bytes 18874368 | tf_op jit(solution)/shard_map/pallas_call | solution.py:103
  70.4 1.9 %slice_bitcast_fusion = bf16[2,256,2048]{2,1,0:T(8,128)(2,1)S(1)} fusion(bf16[2,2,256,2048]{3,2,1,0:T(8,128)(2,1)} %shard_map.64), kind=kLoop, calls=%fused_computation | loop fusion | bytes 4194304 | tf_op jit(solution)/shard_map/squeeze | solution.py:135
  72.5 4.0 %collective-permute-done.8 = bf16[2,256,2048]{2,1,0:T(8,128)(2,1)S(1)} collective-permute-done((bf16[2,256,2048]{2,1,0:T(8,128)(2,1)S(1)}, bf16[2,256,2048]{2,1,0:T(8,128)(2,1)S(1)}, u32[]{:S(2)}, u32[]{:S(2)}) %collective-permute-start.8) | collective-permute-done | bytes 2097184 | tf_op jit(solution)/shard_map/ppermute | solution.py:135
  77.4 1.6 %collective-permute-start.14 = (bf16[64,2048]{1,0:T(8,128)(2,1)S(1)}, bf16[64,2048]{1,0:T(8,128)(2,1)S(1)}, u32[]{:S(2)}, u32[]{:S(2)}) collective-permute-start(bf16[64,2048]{1,0:T(8,128)(2,1)S(1)} %get-tuple-element.11), channel_id=1, source_target_pairs={{0,2},{2,0},{1,3},{3,1},{4,6},{6,4},{5,7},{7,5},{8,10},{10,8},{9,1... | collective-permute-start | bytes 786440 | tf_op jit(solution)/shard_map/ppermute | solution.py:142
  79.5 1.5 %collective-permute-start.10 = (bf16[64,2048]{1,0:T(8,128)(2,1)S(1)}, bf16[64,2048]{1,0:T(8,128)(2,1)S(1)}, u32[]{:S(2)}, u32[]{:S(2)}) collective-permute-start(bf16[64,2048]{1,0:T(8,128)(2,1)S(1)} %get-tuple-element.13), channel_id=1, source_target_pairs={{0,2},{2,0},{1,3},{3,1},{4,6},{6,4},{5,7},{7,5},{8,10},{10,8},{9,1... | collective-permute-start | bytes 786440 | tf_op jit(solution)/shard_map/ppermute | solution.py:142
  81.5 5.1 %collective-permute-done.14 = bf16[64,2048]{1,0:T(8,128)(2,1)S(1)} collective-permute-done((bf16[64,2048]{1,0:T(8,128)(2,1)S(1)}, bf16[64,2048]{1,0:T(8,128)(2,1)S(1)}, u32[]{:S(2)}, u32[]{:S(2)}) %collective-permute-start.14) | collective-permute-done | bytes 262176 | tf_op jit(solution)/shard_map/ppermute | solution.py:142
  86.6 5.6 %collective-permute-done.12 = bf16[64,2048]{1,0:T(8,128)(2,1)S(1)} collective-permute-done((bf16[64,2048]{1,0:T(8,128)(2,1)S(1)}, bf16[64,2048]{1,0:T(8,128)(2,1)S(1)}, u32[]{:S(2)}, u32[]{:S(2)}) %collective-permute-start.12) | collective-permute-done | bytes 262176 | tf_op jit(solution)/shard_map/ppermute | solution.py:142
  92.2 5.6 %collective-permute-done.10 = bf16[64,2048]{1,0:T(8,128)(2,1)S(1)} collective-permute-done((bf16[64,2048]{1,0:T(8,128)(2,1)S(1)}, bf16[64,2048]{1,0:T(8,128)(2,1)S(1)}, u32[]{:S(2)}, u32[]{:S(2)}) %collective-permute-start.10) | collective-permute-done | bytes 262176 | tf_op jit(solution)/shard_map/ppermute | solution.py:142
  98.1 2.0 %collective-permute-start.15 = (bf16[64,2048]{1,0:T(8,128)(2,1)S(1)}, bf16[64,2048]{1,0:T(8,128)(2,1)S(1)}, u32[]{:S(2)}, u32[]{:S(2)}) collective-permute-start(bf16[64,2048]{1,0:T(8,128)(2,1)S(1)} %get-tuple-element.8), channel_id=1, source_target_pairs={{0,4},{4,8},{8,12},{12,0},{1,5},{5,9},{9,13},{13,1},{2,6},{6,10},{... | collective-permute-start | bytes 786440 | tf_op jit(solution)/shard_map/ppermute | solution.py:144
  100.1 2.5 %collective-permute-done.9 = bf16[64,2048]{1,0:T(8,128)(2,1)S(1)} collective-permute-done((bf16[64,2048]{1,0:T(8,128)(2,1)S(1)}, bf16[64,2048]{1,0:T(8,128)(2,1)S(1)}, u32[]{:S(2)}, u32[]{:S(2)}) %collective-permute-start.9) | collective-permute-done | bytes 262176 | tf_op jit(solution)/shard_map/ppermute | solution.py:142
  102.7 8.8 %collective-permute-done.11 = bf16[64,2048]{1,0:T(8,128)(2,1)S(1)} collective-permute-done((bf16[64,2048]{1,0:T(8,128)(2,1)S(1)}, bf16[64,2048]{1,0:T(8,128)(2,1)S(1)}, u32[]{:S(2)}, u32[]{:S(2)}) %collective-permute-start.11) | collective-permute-done | bytes 262176 | tf_op jit(solution)/shard_map/ppermute | solution.py:144
  112.0 7.4 %collective-permute-done.13 = bf16[64,2048]{1,0:T(8,128)(2,1)S(1)} collective-permute-done((bf16[64,2048]{1,0:T(8,128)(2,1)S(1)}, bf16[64,2048]{1,0:T(8,128)(2,1)S(1)}, u32[]{:S(2)}, u32[]{:S(2)}) %collective-permute-start.13) | collective-permute-done | bytes 262176 | tf_op jit(solution)/shard_map/ppermute | solution.py:144
  119.5 0.9 fusion.7
  (28 shorter events, 5.3 us)
Async XLA Ops:
  2.4 12.2 %collective-permute-start.2 = (bf16[64,2176]{1,0:T(8,128)(2,1)S(1)}, bf16[64,2176]{1,0:T(8,128)(2,1)S(1)}, u32[]{:S(2)}, u32[]{:S(2)}) collective-permute-start(bf16[64,2176]{1,0:T(8,128)(2,1)S(1)} %pad_maximum_fusion), channel_id=1, source_target_pairs={{0,12},{4,0},{8,4},{12,8},{1,13},{5,1},{9,5},{13,9},{2,14},{6,2},{... | collective-permute-start | bytes 835592 | tf_op jit(solution)/shard_map/ppermute | solution.py:129
  7.5 23.7 %collective-permute-start.1 = (bf16[64,2176]{1,0:T(8,128)(2,1)S(1)}, bf16[64,2176]{1,0:T(8,128)(2,1)S(1)}, u32[]{:S(2)}, u32[]{:S(2)}) collective-permute-start(bf16[64,2176]{1,0:T(8,128)(2,1)S(1)} %pad_maximum_fusion), channel_id=1, source_target_pairs={{0,8},{4,12},{8,0},{12,4},{1,9},{5,13},{9,1},{13,5},{2,10},{6,14},... | collective-permute-start | bytes 835592 | tf_op jit(solution)/shard_map/ppermute | solution.py:129
  7.5 25.2 %collective-permute-start = (bf16[64,2176]{1,0:T(8,128)(2,1)S(1)}, bf16[64,2176]{1,0:T(8,128)(2,1)S(1)}, u32[]{:S(2)}, u32[]{:S(2)}) collective-permute-start(bf16[64,2176]{1,0:T(8,128)(2,1)S(1)} %pad_maximum_fusion), channel_id=1, source_target_pairs={{0,4},{4,8},{8,12},{12,0},{1,5},{5,9},{9,13},{13,1},{2,6},{6,10},{... | collective-permute-start | bytes 835592 | tf_op jit(solution)/shard_map/ppermute | solution.py:129
  8.5 24.8 %collective-permute-start.3 = (bf16[64,2176]{1,0:T(8,128)(2,1)S(1)}, bf16[64,2176]{1,0:T(8,128)(2,1)S(1)}, u32[]{:S(2)}, u32[]{:S(2)}) collective-permute-start(bf16[64,2176]{1,0:T(8,128)(2,1)S(1)} %pad_maximum_fusion), channel_id=1, source_target_pairs={{0,2},{2,0},{1,3},{3,1},{4,6},{6,4},{5,7},{7,5},{8,10},{10,8},{9,1... | collective-permute-start | bytes 835592 | tf_op jit(solution)/shard_map/ppermute | solution.py:130
  14.6 30.2 %collective-permute-start.6 = (bf16[64,2176]{1,0:T(8,128)(2,1)S(1)}, bf16[64,2176]{1,0:T(8,128)(2,1)S(1)}, u32[]{:S(2)}, u32[]{:S(2)}) collective-permute-start(bf16[64,2176]{1,0:T(8,128)(2,1)S(1)} %collective-permute-done.2), channel_id=1, source_target_pairs={{0,2},{2,0},{1,3},{3,1},{4,6},{6,4},{5,7},{7,5},{8,10},{10,8},{9,1... | collective-permute-start | bytes 835592 | tf_op jit(solution)/shard_map/ppermute | solution.py:130
  31.2 13.5 %collective-permute-start.5 = (bf16[64,2176]{1,0:T(8,128)(2,1)S(1)}, bf16[64,2176]{1,0:T(8,128)(2,1)S(1)}, u32[]{:S(2)}, u32[]{:S(2)}) collective-permute-start(bf16[64,2176]{1,0:T(8,128)(2,1)S(1)} %collective-permute-done.1), channel_id=1, source_target_pairs={{0,2},{2,0},{1,3},{3,1},{4,6},{6,4},{5,7},{7,5},{8,10},{10,8},{9,1... | collective-permute-start | bytes 835592 | tf_op jit(solution)/shard_map/ppermute | solution.py:130
  32.7 12.0 %collective-permute-start.4 = (bf16[64,2176]{1,0:T(8,128)(2,1)S(1)}, bf16[64,2176]{1,0:T(8,128)(2,1)S(1)}, u32[]{:S(2)}, u32[]{:S(2)}) collective-permute-start(bf16[64,2176]{1,0:T(8,128)(2,1)S(1)} %collective-permute-done), channel_id=1, source_target_pairs={{0,2},{2,0},{1,3},{3,1},{4,6},{6,4},{5,7},{7,5},{8,10},{10,8},{9,1... | collective-permute-start | bytes 835592 | tf_op jit(solution)/shard_map/ppermute | solution.py:130
  44.8 4.5 %collective-permute-start.7 = (bf16[2,256,2176]{2,1,0:T(8,128)(2,1)S(1)}, bf16[2,256,2176]{2,1,0:T(8,128)(2,1)}, u32[]{:S(2)}, u32[]{:S(2)}) collective-permute-start(bf16[2,256,2176]{2,1,0:T(8,128)(2,1)S(1)} %bitcast.44), channel_id=1, source_target_pairs={{0,1},{1,0},{2,3},{3,2},{4,5},{5,4},{6,7},{7,6},{8,9},{9,8},{10,11... | collective-permute-start | bytes 6684680 | tf_op jit(solution)/shard_map/ppermute | solution.py:132
  70.4 6.1 %copy-start = (bf16[2,2,256,2048]{3,2,1,0:T(8,128)(2,1)S(1)}, bf16[2,2,256,2048]{3,2,1,0:T(8,128)(2,1)}, u32[]{:S(2)}) copy-start(bf16[2,2,256,2048]{3,2,1,0:T(8,128)(2,1)} %shard_map.64) | copy-start | bytes 12582916
  72.2 4.2 %collective-permute-start.8 = (bf16[2,256,2048]{2,1,0:T(8,128)(2,1)S(1)}, bf16[2,256,2048]{2,1,0:T(8,128)(2,1)S(1)}, u32[]{:S(2)}, u32[]{:S(2)}) collective-permute-start(bf16[2,256,2048]{2,1,0:T(8,128)(2,1)S(1)} %slice_bitcast_fusion), channel_id=1, source_target_pairs={{0,1},{1,0},{2,3},{3,2},{4,5},{5,4},{6,7},{7,6},{8,9},{9,8},{10,11... | collective-permute-start | bytes 6291464 | tf_op jit(solution)/shard_map/ppermute | solution.py:135
  77.4 9.2 %collective-permute-start.14 = (bf16[64,2048]{1,0:T(8,128)(2,1)S(1)}, bf16[64,2048]{1,0:T(8,128)(2,1)S(1)}, u32[]{:S(2)}, u32[]{:S(2)}) collective-permute-start(bf16[64,2048]{1,0:T(8,128)(2,1)S(1)} %get-tuple-element.11), channel_id=1, source_target_pairs={{0,2},{2,0},{1,3},{3,1},{4,6},{6,4},{5,7},{7,5},{8,10},{10,8},{9,1... | collective-permute-start | bytes 786440 | tf_op jit(solution)/shard_map/ppermute | solution.py:142
  79.0 13.2 %collective-permute-start.12 = (bf16[64,2048]{1,0:T(8,128)(2,1)S(1)}, bf16[64,2048]{1,0:T(8,128)(2,1)S(1)}, u32[]{:S(2)}, u32[]{:S(2)}) collective-permute-start(bf16[64,2048]{1,0:T(8,128)(2,1)S(1)} %get-tuple-element.12), channel_id=1, source_target_pairs={{0,2},{2,0},{1,3},{3,1},{4,6},{6,4},{5,7},{7,5},{8,10},{10,8},{9,1... | collective-permute-start | bytes 786440 | tf_op jit(solution)/shard_map/ppermute | solution.py:142
  79.5 18.4 %collective-permute-start.10 = (bf16[64,2048]{1,0:T(8,128)(2,1)S(1)}, bf16[64,2048]{1,0:T(8,128)(2,1)S(1)}, u32[]{:S(2)}, u32[]{:S(2)}) collective-permute-start(bf16[64,2048]{1,0:T(8,128)(2,1)S(1)} %get-tuple-element.13), channel_id=1, source_target_pairs={{0,2},{2,0},{1,3},{3,1},{4,6},{6,4},{5,7},{7,5},{8,10},{10,8},{9,1... | collective-permute-start | bytes 786440 | tf_op jit(solution)/shard_map/ppermute | solution.py:142
  81.0 21.7 %collective-permute-start.9 = (bf16[64,2048]{1,0:T(8,128)(2,1)S(1)}, bf16[64,2048]{1,0:T(8,128)(2,1)S(1)}, u32[]{:S(2)}, u32[]{:S(2)}) collective-permute-start(bf16[64,2048]{1,0:T(8,128)(2,1)S(1)} %get-tuple-element.10), channel_id=1, source_target_pairs={{0,2},{2,0},{1,3},{3,1},{4,6},{6,4},{5,7},{7,5},{8,10},{10,8},{9,1... | collective-permute-start | bytes 786440 | tf_op jit(solution)/shard_map/ppermute | solution.py:142
  98.0 13.4 %collective-permute-start.11 = (bf16[64,2048]{1,0:T(8,128)(2,1)S(1)}, bf16[64,2048]{1,0:T(8,128)(2,1)S(1)}, u32[]{:S(2)}, u32[]{:S(2)}) collective-permute-start(bf16[64,2048]{1,0:T(8,128)(2,1)S(1)} %get-tuple-element.7), channel_id=1, source_target_pairs={{0,12},{4,0},{8,4},{12,8},{1,13},{5,1},{9,5},{13,9},{2,14},{6,2},{... | collective-permute-start | bytes 786440 | tf_op jit(solution)/shard_map/ppermute | solution.py:144
  98.1 13.9 %collective-permute-start.15 = (bf16[64,2048]{1,0:T(8,128)(2,1)S(1)}, bf16[64,2048]{1,0:T(8,128)(2,1)S(1)}, u32[]{:S(2)}, u32[]{:S(2)}) collective-permute-start(bf16[64,2048]{1,0:T(8,128)(2,1)S(1)} %get-tuple-element.8), channel_id=1, source_target_pairs={{0,4},{4,8},{8,12},{12,0},{1,5},{5,9},{9,13},{13,1},{2,6},{6,10},{... | collective-permute-start | bytes 786440 | tf_op jit(solution)/shard_map/ppermute | solution.py:144
  100.1 19.3 %collective-permute-start.13 = (bf16[64,2048]{1,0:T(8,128)(2,1)S(1)}, bf16[64,2048]{1,0:T(8,128)(2,1)S(1)}, u32[]{:S(2)}, u32[]{:S(2)}) collective-permute-start(bf16[64,2048]{1,0:T(8,128)(2,1)S(1)} %get-tuple-element.9), channel_id=1, source_target_pairs={{0,8},{4,12},{8,0},{12,4},{1,9},{5,13},{9,1},{13,5},{2,10},{6,14},... | collective-permute-start | bytes 786440 | tf_op jit(solution)/shard_map/ppermute | solution.py:144

commit v2 on v0

--- a/solution.py
+++ b/solution.py
@@ -1,7 +1,13 @@
+import functools
+
 import jax
 import jax.numpy as jnp
 from jax import lax
+from jax.experimental import pallas as pl
+from jax.experimental.pallas import tpu as pltpu
 from jax.sharding import PartitionSpec as P
+
+LANES = 128
 
 
 def slot_positions(ids_block, experts, capacity):
@@ -12,7 +18,7 @@
     return (flat_ids * capacity + slot_idx).reshape(ids_block.shape)
 
 
-def on_device(tokens, expert_ids, gate_values, w_gate, w_up, w_down):
+def by_slots(tokens, expert_ids, gate_values, w_gate, w_up, w_down):
     peer_count = lax.axis_size(("ep", "sub"))
     tok_rows = tokens.shape[0]
     top_count = expert_ids.shape[1]
@@ -50,6 +56,138 @@
     return mixed.astype(jnp.bfloat16)
 
 
+def expert_kernel(count, after, resident, where_ref, *refs):
+    refs = refs[after:]
+    pieces, refs = refs[: 4 * count], refs[4 * count:]
+    if resident:
+        gate_ref, up_ref, down_ref, mine_ref, cross_ref, x_ref, hidden_ref, scale_ref = refs
+    else:
+        from_refs, (mine_ref, cross_ref, gate_ref, up_ref, down_ref, x_ref, hidden_ref, scale_ref, sems) = refs[:3], refs[3:]
+    depth, width = gate_ref.shape
+    half = depth // 2
+    rows = pieces[0].shape[0]
+    tile = 256 if width % 256 == 0 else width
+    tiles = width // tile
+    down_parts = 4
+    out_tile = depth // down_parts // 2
+    tp, expert = where_ref[0], where_ref[1]
+    starts = [pl.multiple_of(h * half, half) for h in (tp, 1 - tp)]
+    copies = []
+    if not resident:
+        for j in range(tiles):
+            columns = pl.ds(j * tile, tile)
+            copies += [
+                pltpu.make_async_copy(source.at[:, columns], target.at[:, columns], sems.at[2 * j + i])
+                for i, (source, target) in enumerate(zip(from_refs[:2], (gate_ref, up_ref)))
+            ]
+        for i in range(down_parts):
+            h = i // (down_parts // 2)
+            columns = pl.ds(pl.multiple_of(starts[1 - h] + (i % (down_parts // 2)) * 2 * out_tile, out_tile), 2 * out_tile)
+            copies.append(
+                pltpu.make_async_copy(from_refs[2].at[:, columns], down_ref.at[:, columns], sems.at[2 * tiles + i])
+            )
+        for copy in copies:
+            copy.start()
+    lane = lax.broadcasted_iota(jnp.int32, (rows, LANES), 1)
+    for at in range(2 * count):
+        row = pl.ds(at * rows, rows)
+        own, peer = pieces[2 * at], pieces[2 * at + 1]
+        weights = own[:, half:].astype(jnp.float32)
+        scale_ref[row, :] = jnp.sum(jnp.where(lane == expert, weights, 0.0), axis=1, keepdims=True)
+        x_ref[row, pl.ds(starts[0], half)] = own[:, :half]
+        x_ref[row, pl.ds(starts[1], half)] = peer[:, :half]
+
+    for j in range(tiles):
+        columns = pl.ds(j * tile, tile)
+        for copy in copies[2 * j: 2 * j + 2]:
+            copy.wait()
+        gate = jnp.dot(x_ref[...], gate_ref[:, columns], preferred_element_type=jnp.float32)
+        up = jnp.dot(x_ref[...], up_ref[:, columns], preferred_element_type=jnp.float32)
+        hidden_ref[:, columns] = (gate / (1.0 + jnp.exp(-gate)) * up).astype(jnp.bfloat16)
+
+    part = count * rows
+    for i in range(down_parts):
+        h = 1 - i // (down_parts // 2)
+        for copy in copies[2 * tiles + i: 2 * tiles + i + 1]:
+            copy.wait()
+        for n in range(2):
+            offset = (i % (down_parts // 2)) * 2 * out_tile + n * out_tile
+            start = pl.multiple_of(starts[h] + offset, out_tile)
+            value = jnp.dot(
+                hidden_ref[...], down_ref[:, pl.ds(start, out_tile)], preferred_element_type=jnp.float32
+            ) * scale_ref[...]
+            mine_ref[h, :, pl.ds(offset, out_tile)] = value[:part]
+            cross_ref[h, :, pl.ds(offset, out_tile)] = value[part:].astype(jnp.bfloat16)
+
+
+def run_expert(where, after, pieces, weights, resident):
+    count = len(pieces) // 4
+    rows, (depth, width) = pieces[0].shape[0], weights[0].shape
+    half = depth // 2
+    vmem = pl.BlockSpec(memory_space=pltpu.VMEM)
+    hbm = pl.BlockSpec(memory_space=pltpu.HBM)
+    held = [] if resident else [pltpu.VMEM(a.shape, a.dtype) for a in weights]
+    if not resident:
+        weights = [pltpu.with_memory_space_constraint(a, pltpu.HBM) for a in weights]
+    return pl.pallas_call(
+        functools.partial(expert_kernel, count, len(after), resident),
+        out_shape=[
+            pltpu.VMEM((2, count * rows, half), jnp.float32),
+            pltpu.VMEM((2, count * rows, half), jnp.bfloat16),
+        ] + held,
+        in_specs=[pl.BlockSpec(memory_space=pltpu.SMEM)]
+        + [pl.BlockSpec(memory_space=pl.ANY)] * len(after)
+        + [vmem] * len(pieces) + [vmem if resident else hbm] * 3,
+        out_specs=[vmem] * (2 + len(held)),
+        scratch_shapes=[
+            pltpu.VMEM((2 * count * rows, depth), jnp.bfloat16),
+            pltpu.VMEM((2 * count * rows, width), jnp.bfloat16),
+            pltpu.VMEM((2 * count * rows, 1), jnp.float32),
+        ] + ([] if resident else [pltpu.SemaphoreType.DMA((2 * max(1, width // 256) + 4,))]),
+        compiler_params=pltpu.CompilerParams(vmem_limit_bytes=12 * 1024 * 1024),
+        cost_estimate=pl.CostEstimate(
+            flops=2 * 2 * count * rows * 3 * depth * width,
+            bytes_accessed=1024 if resident else 3 * depth * width * 2,
+            transcendentals=0,
+        ),
+    )(where, *after, *pieces, *weights)
+
+
+def by_rows(tokens, expert_ids, gate_values, w_gate, w_up, w_down):
+    ep, sub = lax.axis_size("ep"), lax.axis_size("sub")
+    rows, half = tokens.shape
+    swap = [(0, 1), (1, 0)]
+    ahead = lambda k: [(i, (i + k) % ep) for i in range(ep)]
+    lanes = jnp.arange(LANES, dtype=jnp.int32)
+    weights = jnp.sum(
+        jnp.where(expert_ids[:, :, None] == lanes, gate_values.astype(jnp.float32)[:, :, None], 0.0), axis=1
+    )
+    packed = jnp.concatenate([tokens, weights.astype(jnp.bfloat16)], axis=1)
+    where = jnp.stack([lax.axis_index("tp"), lax.axis_index("ep") * sub + lax.axis_index("sub")]).astype(jnp.int32)
+    mine = [packed] + [lax.ppermute(packed, "ep", ahead(k)) for k in range(1, ep)]
+    peers = [lax.ppermute(a, "tp", swap) for a in mine]
+    order = sorted(range(ep), key=lambda k: min(k, ep - k))
+    first = ep // 2
+    held, resident, after, total = [w_gate[0], w_up[0], w_down[0]], False, mine[1:] + peers[ep // 2 + 1:], None
+    for group in (order[:first], order[first:]):
+        own = [a for k in group for a in (mine[k], peers[k])]
+        other = [lax.ppermute(a, "sub", swap) for a in own]
+        result, crossing, *rest = run_expert(where, after, own + other, held, resident)
+        held, resident = (held, True) if resident else (rest, True)
+        crossed = lax.ppermute(crossing, "sub", swap)
+        after = []
+        for i, k in reversed(list(enumerate(group))):
+            at = slice(i * rows, (i + 1) * rows)
+            to_peer = (result[1, at] + crossed[1, at].astype(jnp.float32)).astype(jnp.bfloat16)
+            part = result[0, at] + crossed[0, at].astype(jnp.float32)
+            part = part + lax.ppermute(to_peer, "tp", swap).astype(jnp.float32)
+            after.append(to_peer)
+            if k:
+                part = lax.ppermute(part.astype(jnp.bfloat16), "ep", ahead(-k)).astype(jnp.float32)
+            total = part if total is None else total + part
+    return total.astype(jnp.bfloat16)
+
+
 def solution(mesh):
     in_specs = (
         P(("grp", "ep", "sub"), "tp"),
@@ -60,6 +198,7 @@
         P(("ep", "sub"), "tp", None),
     )
     out_specs = P(("grp", "ep", "sub"), "tp")
+    small = mesh.shape["tp"] == 2 and mesh.shape["sub"] == 2 and mesh.shape["ep"] <= 4
     return jax.shard_map(
-        on_device, mesh=mesh, in_specs=in_specs, out_specs=out_specs, check_vma=False
-    )
+        by_rows if small else by_slots, mesh=mesh, in_specs=in_specs, out_specs=out_specs, check_vma=False
+    )

time: 219 us -> 104 us (0.47)
  blocking collectives: 86.9 us -> 0 us
  waiting for transfers between devices: 90.6 us -> 59.1 us
  starting transfers between devices: 3.82 us -> 25.8 us
  matrix products: 19.7 us -> 0 us
  Pallas kernels: 0 us -> 15.1 us
  between operations: 13.5 us -> 0.12 us
    all_to_all x1 -> x0, blocking collectives: 76.7 us -> none  [on_device(): lax.all_to_all(outgoing, ('ep', 'sub'), split_axis=0, concat_axis=0, tile...]
    all_to_all x1 -> x0, waiting for transfers between devices: 71.3 us -> none  [on_device(): lax.all_to_all(partial_value, ('ep', 'sub'), split_axis=0, concat_axis=0,...]
    ppermute x0 -> x24, waiting for transfers between devices: none -> 59.1 us  [the longest x4 20.5 us: by_rows(): part = part + lax.ppermute(to_peer, 'tp', swap).astype(jnp.float32)]
    ppermute x0 -> x24, starting transfers between devices: none -> 25.8 us  [the longest x3 13.9 us: by_rows(): lax.ppermute(packed, 'ep', ahead(k))]
    dot_general x4 -> x0, matrix products: 19.7 us -> none  [the longest x1 13.3 us: on_device(): jnp.dot(hidden, w_down[0], preferred_element_type=jnp.float32)]
    reduce_scatter x1 -> x0, waiting for transfers between devices: 19.4 us -> none  [on_device(): mixed = lax.psum_scatter(local_sum, 'tp', scatter_dimension=1, tiled=True)]
    pallas_call x0 -> x2, Pallas kernels: none -> 15.1 us  [run_expert(): pl.pallas_call(functools.partial(expert_kernel, count, len(after), reside...]
    all_gather x1 -> x0, blocking collectives: 10.2 us -> none  [on_device(): full_rows = lax.all_gather(tokens, 'tp', axis=1, tiled=True)]
  transfers between devices with their start and end apart: 2 -> 24, of which waited for: 2 -> 10; matrix products, arithmetic and copies ran while one was open for 0% -> 1% of each run, Pallas kernels for 0% -> 0%
where the time goes in v2:
time: 104 us
  waiting for transfers between devices  59.1 us (57%)
  starting transfers between devices  25.8 us (25%)
  Pallas kernels  15.1 us (15%)
  other arithmetic  3.9 us (4%)
    ppermute x4, waiting for transfers between devices, by_rows(): part = part + lax.ppermute(to_peer, 'tp', swap).astype(jnp.float32)  20.5 us
    pallas_call x2, Pallas kernels, run_expert(): pl.pallas_call(functools.partial(expert_kernel, count, len(after), reside...  15.1 us
    ppermute x3, waiting for transfers between devices, by_rows(): lax.ppermute(part.astype(jnp.bfloat16), 'ep', ahead(-k)).astype(jnp.float32)  15 us
    ppermute x3, starting transfers between devices, by_rows(): lax.ppermute(packed, 'ep', ahead(k))  13.9 us
    ppermute x3, waiting for transfers between devices, by_rows(): lax.ppermute(packed, 'ep', ahead(k))  11.4 us
    ppermute x4, waiting for transfers between devices, by_rows(): peers = [lax.ppermute(a, 'tp', swap) for a in mine]  10.2 us
    ppermute x4, starting transfers between devices, by_rows(): peers = [lax.ppermute(a, 'tp', swap) for a in mine]  4.36 us
    ppermute x4, starting transfers between devices, by_rows(): part = part + lax.ppermute(to_peer, 'tp', swap).astype(jnp.float32)  4.16 us
  transfers between devices with their start and end apart: 24, of which 10 were waited for; matrix products, arithmetic and copies ran while one was open for 1% of the time, Pallas kernels for 0%

profile of v2, /device:TPU:0, one launch (start us, length us, event | category | flops | bytes accessed | tf_op | source)
XLA Modules:
  0.0 104.0 jit_solution(12845382072251879852)
XLA Ops:
  0.0 0.7 convert_element_type.93
  0.7 0.8 select_reduce_fusion
  1.4 1.0 pad_maximum_fusion.refs_4_
  2.4 3.1 %collective-permute-start = (bf16[64,2176]{1,0:T(8,128)(2,1)S(1)}, bf16[64,2176]{1,0:T(8,128)(2,1)S(1)}, u32[]{:S(2)}, u32[]{:S(2)}) collective-permute-start(bf16[64,2176]{1,0:T(8,128)(2,1)S(1)} %pad_maximum_fusion.refs_4_), channel_id=1, source_target_pairs={{0,4},{4,8},{8,12},{12,0},{1,5},{5,9},{9,13},{13,1},{2,6},{6,10},{... | collective-permute-start | bytes 835592 | tf_op jit(solution)/shard_map/ppermute | solution.py:167
  5.5 1.5 %collective-permute-start.4 = (bf16[64,2176]{1,0:T(8,128)(2,1)S(1)}, bf16[64,2176]{1,0:T(8,128)(2,1)S(1)}, u32[]{:S(2)}, u32[]{:S(2)}) collective-permute-start(bf16[64,2176]{1,0:T(8,128)(2,1)S(1)} %pad_maximum_fusion.refs_4_), channel_id=1, source_target_pairs={{0,2},{2,0},{1,3},{3,1},{4,6},{6,4},{5,7},{7,5},{8,10},{10,8},{9,1... | collective-permute-start | bytes 835592 | tf_op jit(solution)/shard_map/ppermute | solution.py:168
  7.0 2.2 %collective-permute-start.2 = (bf16[64,2176]{1,0:T(8,128)(2,1)S(1)}, bf16[64,2176]{1,0:T(8,128)(2,1)S(1)}, u32[]{:S(2)}, u32[]{:S(2)}) collective-permute-start(bf16[64,2176]{1,0:T(8,128)(2,1)S(1)} %pad_maximum_fusion.refs_4_), channel_id=1, source_target_pairs={{0,12},{4,0},{8,4},{12,8},{1,13},{5,1},{9,5},{13,9},{2,14},{6,2},{... | collective-permute-start | bytes 835592 | tf_op jit(solution)/shard_map/ppermute | solution.py:167
  9.2 5.8 %collective-permute-done.refs_0_.refs_6_ = bf16[64,2176]{1,0:T(8,128)(2,1)S(1)} collective-permute-done((bf16[64,2176]{1,0:T(8,128)(2,1)S(1)}, bf16[64,2176]{1,0:T(8,128)(2,1)S(1)}, u32[]{:S(2)}, u32[]{:S(2)}) %collective-permute-start) | collective-permute-done | bytes 278560 | tf_op jit(solution)/shard_map/ppermute | solution.py:167
  15.0 1.7 %collective-permute-start.5 = (bf16[64,2176]{1,0:T(8,128)(2,1)S(1)}, bf16[64,2176]{1,0:T(8,128)(2,1)S(1)}, u32[]{:S(2)}, u32[]{:S(2)}) collective-permute-start(bf16[64,2176]{1,0:T(8,128)(2,1)S(1)} %collective-permute-done.refs_0_.refs_6_), channel_id=1, source_target_pairs={{0,2},{2,0},{1,3},{3,1},{4,6},{6,4},{5,7},{7,5},{8,10},{10,8},{9,1... | collective-permute-start | bytes 835592 | tf_op jit(solution)/shard_map/ppermute | solution.py:168
  16.8 8.6 %collective-permute-start.1 = (bf16[64,2176]{1,0:T(8,128)(2,1)S(1)}, bf16[64,2176]{1,0:T(8,128)(2,1)S(1)}, u32[]{:S(2)}, u32[]{:S(2)}) collective-permute-start(bf16[64,2176]{1,0:T(8,128)(2,1)S(1)} %pad_maximum_fusion.refs_4_), channel_id=1, source_target_pairs={{0,8},{4,12},{8,0},{12,4},{1,9},{5,13},{9,1},{13,5},{2,10},{6,14},... | collective-permute-start | bytes 835592 | tf_op jit(solution)/shard_map/ppermute | solution.py:167
  26.5 5.6 %collective-permute-done.1.refs_1_.refs_4_ = bf16[64,2176]{1,0:T(8,128)(2,1)S(1)} collective-permute-done((bf16[64,2176]{1,0:T(8,128)(2,1)S(1)}, bf16[64,2176]{1,0:T(8,128)(2,1)S(1)}, u32[]{:S(2)}, u32[]{:S(2)}) %collective-permute-start.1) | collective-permute-done | bytes 278560 | tf_op jit(solution)/shard_map/ppermute | solution.py:167
  32.1 2.4 %collective-permute-done.3.refs_3_ = bf16[64,2176]{1,0:T(8,128)(2,1)S(1)} collective-permute-done((bf16[64,2176]{1,0:T(8,128)(2,1)S(1)}, bf16[64,2176]{1,0:T(8,128)(2,1)S(1)}, u32[]{:S(2)}, u32[]{:S(2)}) %collective-permute-start.3) | collective-permute-done | bytes 278560 | tf_op jit(solution)/shard_map/ppermute | solution.py:168
  34.5 9.1 %shard_map.64 = (f32[2,128,2048]{2,1,0:T(8,128)S(1)}, bf16[2,128,2048]{2,1,0:T(8,128)(2,1)S(1)}, bf16[4096,768]{1,0:T(8,128)(2,1)S(1)}, bf16[4096,768]{1,0:T(8,128)(2,1)S(1)}, bf16[768,4096]{1,0:T(8,128)(2,1)S(1)}) custom-call(s32[2]{0:T(128)S(1)} %pad_add_fusion.where_ref, bf16[64,2176]{1,0:T(8,128)(2,1)S(1)} %collective-permute-done.refs_0_.refs_6_, ...), custom_call_target="tpu_custom_call" | custom-call | flops 4831838208 | bytes 18874368 | tf_op jit(solution)/shard_map/pallas_call | solution.py:132
  43.7 0.6 collective-permute-start.14
  45.0 7.8 %collective-permute-done.14.refs_5_ = bf16[64,2176]{1,0:T(8,128)(2,1)S(1)} collective-permute-done((bf16[64,2176]{1,0:T(8,128)(2,1)S(1)}, bf16[64,2176]{1,0:T(8,128)(2,1)S(1)}, u32[]{:S(2)}, u32[]{:S(2)}) %collective-permute-start.14) | collective-permute-done | bytes 278560 | tf_op jit(solution)/shard_map/ppermute | solution.py:168
  53.0 1.4 %collective-permute-done.18.refs_9_ = bf16[64,2176]{1,0:T(8,128)(2,1)S(1)} collective-permute-done((bf16[64,2176]{1,0:T(8,128)(2,1)S(1)}, bf16[64,2176]{1,0:T(8,128)(2,1)S(1)}, u32[]{:S(2)}, u32[]{:S(2)}) %collective-permute-start.18) | collective-permute-done | bytes 278560 | tf_op jit(solution)/shard_map/ppermute | solution.py:174
  54.3 5.9 %shard_map.65 = (f32[2,128,2048]{2,1,0:T(8,128)S(1)}, bf16[2,128,2048]{2,1,0:T(8,128)(2,1)S(1)}) custom-call(s32[2]{0:T(128)S(1)} %pad_add_fusion.where_ref, bf16[64,2048]{1,0:T(8,128)(2,1)S(1)} %get-tuple-element.24.refs_0_, bf16[64,2048]{1,0:T(8,128)(2,1)S(1)} %get-tuple-element.23.refs_1_, bf16[64,2176]{1,0:T(8,128)(2,1)S(1)} %collective-permute-done.2.refs_2_, ...), custom_call_target="tpu_custom_call" | custom-call | flops 4831838208 | bytes 1024 | tf_op jit(solution)/shard_map/pallas_call | solution.py:132
  61.0 1.5 %collective-permute-start.11 = (bf16[64,2048]{1,0:T(8,128)(2,1)S(1)}, bf16[64,2048]{1,0:T(8,128)(2,1)S(1)}, u32[]{:S(2)}, u32[]{:S(2)}) collective-permute-start(bf16[64,2048]{1,0:T(8,128)(2,1)S(1)} %get-tuple-element.24.refs_0_), channel_id=1, source_target_pairs={{0,2},{2,0},{1,3},{3,1},{4,6},{6,4},{5,7},{7,5},{8,10},{10,8},{9,1... | collective-permute-start | bytes 786440 | tf_op jit(solution)/shard_map/ppermute | solution.py:183
  63.7 1.5 %collective-permute-start.22 = (bf16[64,2048]{1,0:T(8,128)(2,1)S(1)}, bf16[64,2048]{1,0:T(8,128)(2,1)S(1)}, u32[]{:S(2)}, u32[]{:S(2)}) collective-permute-start(bf16[64,2048]{1,0:T(8,128)(2,1)S(1)} %get-tuple-element.22), channel_id=1, source_target_pairs={{0,2},{2,0},{1,3},{3,1},{4,6},{6,4},{5,7},{7,5},{8,10},{10,8},{9,1... | collective-permute-start | bytes 786440 | tf_op jit(solution)/shard_map/ppermute | solution.py:183
  65.2 10.0 %collective-permute-done.11 = bf16[64,2048]{1,0:T(8,128)(2,1)S(1)} collective-permute-done((bf16[64,2048]{1,0:T(8,128)(2,1)S(1)}, bf16[64,2048]{1,0:T(8,128)(2,1)S(1)}, u32[]{:S(2)}, u32[]{:S(2)}) %collective-permute-start.11) | collective-permute-done | bytes 262176 | tf_op jit(solution)/shard_map/ppermute | solution.py:183
  75.4 5.4 %collective-permute-done.20 = bf16[64,2048]{1,0:T(8,128)(2,1)S(1)} collective-permute-done((bf16[64,2048]{1,0:T(8,128)(2,1)S(1)}, bf16[64,2048]{1,0:T(8,128)(2,1)S(1)}, u32[]{:S(2)}, u32[]{:S(2)}) %collective-permute-start.20) | collective-permute-done | bytes 262176 | tf_op jit(solution)/shard_map/ppermute | solution.py:183
  80.9 5.1 %collective-permute-done.22 = bf16[64,2048]{1,0:T(8,128)(2,1)S(1)} collective-permute-done((bf16[64,2048]{1,0:T(8,128)(2,1)S(1)}, bf16[64,2048]{1,0:T(8,128)(2,1)S(1)}, u32[]{:S(2)}, u32[]{:S(2)}) %collective-permute-start.22) | collective-permute-done | bytes 262176 | tf_op jit(solution)/shard_map/ppermute | solution.py:183
  86.1 1.9 %collective-permute-start.21 = (bf16[64,2048]{1,0:T(8,128)(2,1)S(1)}, bf16[64,2048]{1,0:T(8,128)(2,1)S(1)}, u32[]{:S(2)}, u32[]{:S(2)}) collective-permute-start(bf16[64,2048]{1,0:T(8,128)(2,1)S(1)} %get-tuple-element.19), channel_id=1, source_target_pairs={{0,8},{4,12},{8,0},{12,4},{1,9},{5,13},{9,1},{13,5},{2,10},{6,14},... | collective-permute-start | bytes 786440 | tf_op jit(solution)/shard_map/ppermute | solution.py:186
  88.1 15.0 %collective-permute-done.21 = bf16[64,2048]{1,0:T(8,128)(2,1)S(1)} collective-permute-done((bf16[64,2048]{1,0:T(8,128)(2,1)S(1)}, bf16[64,2048]{1,0:T(8,128)(2,1)S(1)}, u32[]{:S(2)}, u32[]{:S(2)}) %collective-permute-start.21) | collective-permute-done | bytes 262176 | tf_op jit(solution)/shard_map/ppermute | solution.py:186
  103.1 0.9 fusion.5
  (35 shorter events, 4.3 us)
Async XLA Ops:
  2.4 12.6 %collective-permute-start = (bf16[64,2176]{1,0:T(8,128)(2,1)S(1)}, bf16[64,2176]{1,0:T(8,128)(2,1)S(1)}, u32[]{:S(2)}, u32[]{:S(2)}) collective-permute-start(bf16[64,2176]{1,0:T(8,128)(2,1)S(1)} %pad_maximum_fusion.refs_4_), channel_id=1, source_target_pairs={{0,4},{4,8},{8,12},{12,0},{1,5},{5,9},{9,13},{13,1},{2,6},{6,10},{... | collective-permute-start | bytes 835592 | tf_op jit(solution)/shard_map/ppermute | solution.py:167
  5.5 19.9 %collective-permute-start.6 = (bf16[64,2176]{1,0:T(8,128)(2,1)S(1)}, bf16[64,2176]{1,0:T(8,128)(2,1)S(1)}, u32[]{:S(2)}, u32[]{:S(2)}) collective-permute-start(bf16[64,2176]{1,0:T(8,128)(2,1)S(1)} %pad_maximum_fusion.refs_4_), channel_id=1, source_target_pairs={{0,1},{1,0},{2,3},{3,2},{4,5},{5,4},{6,7},{7,6},{8,9},{9,8},{10,11... | collective-permute-start | bytes 835592 | tf_op jit(solution)/shard_map/ppermute | solution.py:174
  5.5 19.9 %collective-permute-start.4 = (bf16[64,2176]{1,0:T(8,128)(2,1)S(1)}, bf16[64,2176]{1,0:T(8,128)(2,1)S(1)}, u32[]{:S(2)}, u32[]{:S(2)}) collective-permute-start(bf16[64,2176]{1,0:T(8,128)(2,1)S(1)} %pad_maximum_fusion.refs_4_), channel_id=1, source_target_pairs={{0,2},{2,0},{1,3},{3,1},{4,6},{6,4},{5,7},{7,5},{8,10},{10,8},{9,1... | collective-permute-start | bytes 835592 | tf_op jit(solution)/shard_map/ppermute | solution.py:168
  7.0 18.9 %collective-permute-start.2 = (bf16[64,2176]{1,0:T(8,128)(2,1)S(1)}, bf16[64,2176]{1,0:T(8,128)(2,1)S(1)}, u32[]{:S(2)}, u32[]{:S(2)}) collective-permute-start(bf16[64,2176]{1,0:T(8,128)(2,1)S(1)} %pad_maximum_fusion.refs_4_), channel_id=1, source_target_pairs={{0,12},{4,0},{8,4},{12,8},{1,13},{5,1},{9,5},{13,9},{2,14},{6,2},{... | collective-permute-start | bytes 835592 | tf_op jit(solution)/shard_map/ppermute | solution.py:167
  15.0 11.4 %collective-permute-start.5 = (bf16[64,2176]{1,0:T(8,128)(2,1)S(1)}, bf16[64,2176]{1,0:T(8,128)(2,1)S(1)}, u32[]{:S(2)}, u32[]{:S(2)}) collective-permute-start(bf16[64,2176]{1,0:T(8,128)(2,1)S(1)} %collective-permute-done.refs_0_.refs_6_), channel_id=1, source_target_pairs={{0,2},{2,0},{1,3},{3,1},{4,6},{6,4},{5,7},{7,5},{8,10},{10,8},{9,1... | collective-permute-start | bytes 835592 | tf_op jit(solution)/shard_map/ppermute | solution.py:168
  16.8 15.3 %collective-permute-start.1 = (bf16[64,2176]{1,0:T(8,128)(2,1)S(1)}, bf16[64,2176]{1,0:T(8,128)(2,1)S(1)}, u32[]{:S(2)}, u32[]{:S(2)}) collective-permute-start(bf16[64,2176]{1,0:T(8,128)(2,1)S(1)} %pad_maximum_fusion.refs_4_), channel_id=1, source_target_pairs={{0,8},{4,12},{8,0},{12,4},{1,9},{5,13},{9,1},{13,5},{2,10},{6,14},... | collective-permute-start | bytes 835592 | tf_op jit(solution)/shard_map/ppermute | solution.py:167
  25.4 9.2 %collective-permute-start.8 = (bf16[64,2176]{1,0:T(8,128)(2,1)S(1)}, bf16[64,2176]{1,0:T(8,128)(2,1)S(1)}, u32[]{:S(2)}, u32[]{:S(2)}) collective-permute-start(bf16[64,2176]{1,0:T(8,128)(2,1)S(1)} %collective-permute-done.refs_0_.refs_6_), channel_id=1, source_target_pairs={{0,1},{1,0},{2,3},{3,2},{4,5},{5,4},{6,7},{7,6},{8,9},{9,8},{10,11... | collective-permute-start | bytes 835592 | tf_op jit(solution)/shard_map/ppermute | solution.py:174
  25.4 6.7 %collective-permute-start.7 = (bf16[64,2176]{1,0:T(8,128)(2,1)S(1)}, bf16[64,2176]{1,0:T(8,128)(2,1)S(1)}, u32[]{:S(2)}, u32[]{:S(2)}) collective-permute-start(bf16[64,2176]{1,0:T(8,128)(2,1)S(1)} %collective-permute-done.4.refs_5_), channel_id=1, source_target_pairs={{0,1},{1,0},{2,3},{3,2},{4,5},{5,4},{6,7},{7,6},{8,9},{9,8},{10,11... | collective-permute-start | bytes 835592 | tf_op jit(solution)/shard_map/ppermute | solution.py:174
  25.9 8.6 %collective-permute-start.3 = (bf16[64,2176]{1,0:T(8,128)(2,1)S(1)}, bf16[64,2176]{1,0:T(8,128)(2,1)S(1)}, u32[]{:S(2)}, u32[]{:S(2)}) collective-permute-start(bf16[64,2176]{1,0:T(8,128)(2,1)S(1)} %collective-permute-done.2.refs_2_), channel_id=1, source_target_pairs={{0,2},{2,0},{1,3},{3,1},{4,6},{6,4},{5,7},{7,5},{8,10},{10,8},{9,1... | collective-permute-start | bytes 835592 | tf_op jit(solution)/shard_map/ppermute | solution.py:168
  26.4 8.1 %collective-permute-start.9 = (bf16[64,2176]{1,0:T(8,128)(2,1)S(1)}, bf16[64,2176]{1,0:T(8,128)(2,1)S(1)}, u32[]{:S(2)}, u32[]{:S(2)}) collective-permute-start(bf16[64,2176]{1,0:T(8,128)(2,1)S(1)} %collective-permute-done.5.refs_7_), channel_id=1, source_target_pairs={{0,1},{1,0},{2,3},{3,2},{4,5},{5,4},{6,7},{7,6},{8,9},{9,8},{10,11... | collective-permute-start | bytes 835592 | tf_op jit(solution)/shard_map/ppermute | solution.py:174
  43.6 9.2 %collective-permute-start.10 = (bf16[2,128,2048]{2,1,0:T(8,128)(2,1)S(1)}, bf16[2,128,2048]{2,1,0:T(8,128)(2,1)S(1)}, u32[]{:S(2)}, u32[]{:S(2)}) collective-permute-start(bf16[2,128,2048]{2,1,0:T(8,128)(2,1)S(1)} %get-tuple-element.13), channel_id=1, source_target_pairs={{0,1},{1,0},{2,3},{3,2},{4,5},{5,4},{6,7},{7,6},{8,9},{9,8},{10,11... | collective-permute-start | bytes 3145736 | tf_op jit(solution)/shard_map/ppermute | solution.py:177
  43.7 9.1 %collective-permute-start.14 = (bf16[64,2176]{1,0:T(8,128)(2,1)S(1)}, bf16[64,2176]{1,0:T(8,128)(2,1)S(1)}, u32[]{:S(2)}, u32[]{:S(2)}) collective-permute-start(bf16[64,2176]{1,0:T(8,128)(2,1)S(1)} %collective-permute-done.1.refs_1_.refs_4_), channel_id=1, source_target_pairs={{0,2},{2,0},{1,3},{3,1},{4,6},{6,4},{5,7},{7,5},{8,10},{10,8},{9,1... | collective-permute-start | bytes 835592 | tf_op jit(solution)/shard_map/ppermute | solution.py:168
  44.3 8.6 %collective-permute-start.15 = (bf16[64,2176]{1,0:T(8,128)(2,1)S(1)}, bf16[64,2176]{1,0:T(8,128)(2,1)S(1)}, u32[]{:S(2)}, u32[]{:S(2)}) collective-permute-start(bf16[64,2176]{1,0:T(8,128)(2,1)S(1)} %collective-permute-done.2.refs_2_), channel_id=1, source_target_pairs={{0,1},{1,0},{2,3},{3,2},{4,5},{5,4},{6,7},{7,6},{8,9},{9,8},{10,11... | collective-permute-start | bytes 835592 | tf_op jit(solution)/shard_map/ppermute | solution.py:174
  44.5 8.5 %collective-permute-start.17 = (bf16[64,2176]{1,0:T(8,128)(2,1)S(1)}, bf16[64,2176]{1,0:T(8,128)(2,1)S(1)}, u32[]{:S(2)}, u32[]{:S(2)}) collective-permute-start(bf16[64,2176]{1,0:T(8,128)(2,1)S(1)} %collective-permute-done.1.refs_1_.refs_4_), channel_id=1, source_target_pairs={{0,1},{1,0},{2,3},{3,2},{4,5},{5,4},{6,7},{7,6},{8,9},{9,8},{10,11... | collective-permute-start | bytes 835592 | tf_op jit(solution)/shard_map/ppermute | solution.py:174
  44.8 8.1 %collective-permute-start.16 = (bf16[64,2176]{1,0:T(8,128)(2,1)S(1)}, bf16[64,2176]{1,0:T(8,128)(2,1)S(1)}, u32[]{:S(2)}, u32[]{:S(2)}) collective-permute-start(bf16[64,2176]{1,0:T(8,128)(2,1)S(1)} %collective-permute-done.3.refs_3_), channel_id=1, source_target_pairs={{0,1},{1,0},{2,3},{3,2},{4,5},{5,4},{6,7},{7,6},{8,9},{9,8},{10,11... | collective-permute-start | bytes 835592 | tf_op jit(solution)/shard_map/ppermute | solution.py:174
  52.8 1.6 %collective-permute-start.18 = (bf16[64,2176]{1,0:T(8,128)(2,1)S(1)}, bf16[64,2176]{1,0:T(8,128)(2,1)S(1)}, u32[]{:S(2)}, u32[]{:S(2)}) collective-permute-start(bf16[64,2176]{1,0:T(8,128)(2,1)S(1)} %collective-permute-done.14.refs_5_), channel_id=1, source_target_pairs={{0,1},{1,0},{2,3},{3,2},{4,5},{5,4},{6,7},{7,6},{8,9},{9,8},{10,11... | collective-permute-start | bytes 835592 | tf_op jit(solution)/shard_map/ppermute | solution.py:174
  60.3 2.7 %collective-permute-start.19 = (bf16[2,128,2048]{2,1,0:T(8,128)(2,1)S(1)}, bf16[2,128,2048]{2,1,0:T(8,128)(2,1)S(1)}, u32[]{:S(2)}, u32[]{:S(2)}) collective-permute-start(bf16[2,128,2048]{2,1,0:T(8,128)(2,1)S(1)} %get-tuple-element.18), channel_id=1, source_target_pairs={{0,1},{1,0},{2,3},{3,2},{4,5},{5,4},{6,7},{7,6},{8,9},{9,8},{10,11... | collective-permute-start | bytes 3145736 | tf_op jit(solution)/shard_map/ppermute | solution.py:177
  60.5 27.6 %collective-permute-start.13 = (bf16[64,2048]{1,0:T(8,128)(2,1)S(1)}, bf16[64,2048]{1,0:T(8,128)(2,1)S(1)}, u32[]{:S(2)}, u32[]{:S(2)}) collective-permute-start(bf16[64,2048]{1,0:T(8,128)(2,1)S(1)} %get-tuple-element.23.refs_1_), channel_id=1, source_target_pairs={{0,2},{2,0},{1,3},{3,1},{4,6},{6,4},{5,7},{7,5},{8,10},{10,8},{9,1... | collective-permute-start | bytes 786440 | tf_op jit(solution)/shard_map/ppermute | solution.py:183
  61.0 14.2 %collective-permute-start.11 = (bf16[64,2048]{1,0:T(8,128)(2,1)S(1)}, bf16[64,2048]{1,0:T(8,128)(2,1)S(1)}, u32[]{:S(2)}, u32[]{:S(2)}) collective-permute-start(bf16[64,2048]{1,0:T(8,128)(2,1)S(1)} %get-tuple-element.24.refs_0_), channel_id=1, source_target_pairs={{0,2},{2,0},{1,3},{3,1},{4,6},{6,4},{5,7},{7,5},{8,10},{10,8},{9,1... | collective-permute-start | bytes 786440 | tf_op jit(solution)/shard_map/ppermute | solution.py:183
  63.1 17.7 %collective-permute-start.20 = (bf16[64,2048]{1,0:T(8,128)(2,1)S(1)}, bf16[64,2048]{1,0:T(8,128)(2,1)S(1)}, u32[]{:S(2)}, u32[]{:S(2)}) collective-permute-start(bf16[64,2048]{1,0:T(8,128)(2,1)S(1)} %get-tuple-element.21), channel_id=1, source_target_pairs={{0,2},{2,0},{1,3},{3,1},{4,6},{6,4},{5,7},{7,5},{8,10},{10,8},{9,1... | collective-permute-start | bytes 786440 | tf_op jit(solution)/shard_map/ppermute | solution.py:183
  63.7 22.2 %collective-permute-start.22 = (bf16[64,2048]{1,0:T(8,128)(2,1)S(1)}, bf16[64,2048]{1,0:T(8,128)(2,1)S(1)}, u32[]{:S(2)}, u32[]{:S(2)}) collective-permute-start(bf16[64,2048]{1,0:T(8,128)(2,1)S(1)} %get-tuple-element.22), channel_id=1, source_target_pairs={{0,2},{2,0},{1,3},{3,1},{4,6},{6,4},{5,7},{7,5},{8,10},{10,8},{9,1... | collective-permute-start | bytes 786440 | tf_op jit(solution)/shard_map/ppermute | solution.py:183
  75.4 12.7 %collective-permute-start.12 = (bf16[64,2048]{1,0:T(8,128)(2,1)S(1)}, bf16[64,2048]{1,0:T(8,128)(2,1)S(1)}, u32[]{:S(2)}, u32[]{:S(2)}) collective-permute-start(bf16[64,2048]{1,0:T(8,128)(2,1)S(1)} %fusion.6), channel_id=1, source_target_pairs={{0,12},{4,0},{8,4},{12,8},{1,13},{5,1},{9,5},{13,9},{2,14},{6,2},{... | collective-permute-start | bytes 786440 | tf_op jit(solution)/shard_map/ppermute | solution.py:186
  86.1 17.0 %collective-permute-start.21 = (bf16[64,2048]{1,0:T(8,128)(2,1)S(1)}, bf16[64,2048]{1,0:T(8,128)(2,1)S(1)}, u32[]{:S(2)}, u32[]{:S(2)}) collective-permute-start(bf16[64,2048]{1,0:T(8,128)(2,1)S(1)} %get-tuple-element.19), channel_id=1, source_target_pairs={{0,8},{4,12},{8,0},{12,4},{1,9},{5,13},{9,1},{13,5},{2,10},{6,14},... | collective-permute-start | bytes 786440 | tf_op jit(solution)/shard_map/ppermute | solution.py:186
  88.0 15.0 %collective-permute-start.23 = (bf16[64,2048]{1,0:T(8,128)(2,1)S(1)}, bf16[64,2048]{1,0:T(8,128)(2,1)S(1)}, u32[]{:S(2)}, u32[]{:S(2)}) collective-permute-start(bf16[64,2048]{1,0:T(8,128)(2,1)S(1)} %get-tuple-element.20), channel_id=1, source_target_pairs={{0,4},{4,8},{8,12},{12,0},{1,5},{5,9},{9,13},{13,1},{2,6},{6,10},{... | collective-permute-start | bytes 786440 | tf_op jit(solution)/shard_map/ppermute | solution.py:186

commit v3 on v2

--- a/solution.py
+++ b/solution.py
@@ -54,6 +54,38 @@
     )
     mixed = lax.psum_scatter(local_sum, "tp", scatter_dimension=1, tiled=True)
     return mixed.astype(jnp.bfloat16)
+
+
+def pack_kernel(tokens_ref, ids_hbm_ref, gates_hbm_ref, out_ref, ids_ref, gates_ref, sems):
+    rows, half = tokens_ref.shape
+    copies = [
+        pltpu.make_async_copy(source, target, sems.at[i])
+        for i, (source, target) in enumerate(
+            ((ids_hbm_ref, ids_ref), (gates_hbm_ref, gates_ref), (tokens_ref, out_ref.at[:, pl.ds(0, half)]))
+        )
+    ]
+    for copy in copies:
+        copy.start()
+    for copy in copies[:2]:
+        copy.wait()
+    expert = lax.broadcasted_iota(jnp.int32, (LANES, rows), 0)
+    weights = jnp.zeros((LANES, rows), jnp.float32)
+    for k in range(ids_ref.shape[0]):
+        weights = weights + jnp.where(expert == ids_ref[k:k + 1, :], gates_ref[k:k + 1, :].astype(jnp.float32), 0.0)
+    out_ref[:, half:] = weights.T.astype(jnp.bfloat16)
+    copies[2].wait()
+
+
+def pack(tokens, expert_ids, gate_values):
+    arrays = [pltpu.with_memory_space_constraint(a, pltpu.HBM) for a in (tokens, expert_ids.T, gate_values.T)]
+    return pl.pallas_call(
+        pack_kernel,
+        out_shape=pltpu.VMEM((tokens.shape[0], tokens.shape[1] + LANES), jnp.bfloat16),
+        in_specs=[pl.BlockSpec(memory_space=pltpu.HBM)] * 3,
+        out_specs=pl.BlockSpec(memory_space=pltpu.VMEM),
+        scratch_shapes=[pltpu.VMEM(a.shape, a.dtype) for a in arrays[1:]] + [pltpu.SemaphoreType.DMA((3,))],
+        compiler_params=pltpu.CompilerParams(vmem_limit_bytes=1024 * 1024),
+    )(*arrays)
 
 
 def expert_kernel(count, after, resident, where_ref, *refs):
@@ -153,38 +185,87 @@
     )(where, *after, *pieces, *weights)
 
 
+def add_kernel(h, at, rows, *refs):
+    *refs, result_ref, crossed_ref, out_ref = refs
+    row = pl.ds(at * rows, rows)
+    total = result_ref[h, row, :] + crossed_ref[h, row, :].astype(jnp.float32)
+    for ref in refs:
+        total = total + ref[...].astype(jnp.float32)
+    out_ref[...] = total.astype(out_ref.dtype)
+
+
+def add(h, at, rows, result, crossed, *arrived):
+    vmem = pl.BlockSpec(memory_space=pltpu.VMEM)
+    return pl.pallas_call(
+        functools.partial(add_kernel, h, at, rows),
+        out_shape=pltpu.VMEM((rows, result.shape[2]), jnp.bfloat16),
+        in_specs=[vmem] * (2 + len(arrived)),
+        out_specs=vmem,
+        compiler_params=pltpu.CompilerParams(vmem_limit_bytes=4 * 1024 * 1024),
+        cost_estimate=pl.CostEstimate(flops=0, bytes_accessed=1024, transcendentals=0),
+    )(*arrived, result, crossed)
+
+
+def tie_kernel(*refs):
+    pass
+
+
+def tie_all(arrays, *after):
+    count = len(arrays)
+    return pl.pallas_call(
+        tie_kernel,
+        out_shape=[pltpu.VMEM(a.shape, a.dtype) for a in arrays],
+        in_specs=[pl.BlockSpec(memory_space=pltpu.VMEM)] * count + [pl.BlockSpec(memory_space=pl.ANY)] * len(after),
+        out_specs=[pl.BlockSpec(memory_space=pltpu.VMEM)] * count,
+        input_output_aliases={i: i for i in range(count)},
+        compiler_params=pltpu.CompilerParams(vmem_limit_bytes=1024 * 1024),
+        cost_estimate=pl.CostEstimate(flops=0, bytes_accessed=0, transcendentals=0),
+    )(*arrays, *after)
+
+
+def tie(array, *after):
+    return tie_all([array], *after)[0]
+
+
 def by_rows(tokens, expert_ids, gate_values, w_gate, w_up, w_down):
-    ep, sub = lax.axis_size("ep"), lax.axis_size("sub")
-    rows, half = tokens.shape
+    ep = lax.axis_size("ep")
+    rows = tokens.shape[0]
     swap = [(0, 1), (1, 0)]
     ahead = lambda k: [(i, (i + k) % ep) for i in range(ep)]
-    lanes = jnp.arange(LANES, dtype=jnp.int32)
-    weights = jnp.sum(
-        jnp.where(expert_ids[:, :, None] == lanes, gate_values.astype(jnp.float32)[:, :, None], 0.0), axis=1
-    )
-    packed = jnp.concatenate([tokens, weights.astype(jnp.bfloat16)], axis=1)
-    where = jnp.stack([lax.axis_index("tp"), lax.axis_index("ep") * sub + lax.axis_index("sub")]).astype(jnp.int32)
-    mine = [packed] + [lax.ppermute(packed, "ep", ahead(k)) for k in range(1, ep)]
-    peers = [lax.ppermute(a, "tp", swap) for a in mine]
-    order = sorted(range(ep), key=lambda k: min(k, ep - k))
-    first = ep // 2
-    held, resident, after, total = [w_gate[0], w_up[0], w_down[0]], False, mine[1:] + peers[ep // 2 + 1:], None
-    for group in (order[:first], order[first:]):
+    far = ep // 2
+    second = tuple(k for k in range(1, ep) if k != far)
+    packed = pack(tokens, expert_ids, gate_values)
+    mine = {k: lax.ppermute(packed, "ep", ahead(k)) if k else packed for k in (far, *second, 0)}
+    where = jnp.stack([lax.axis_index("tp"), lax.axis_index("ep") * 2 + lax.axis_index("sub")]).astype(jnp.int32)
+    peers = {0: lax.ppermute(packed, "tp", swap)}
+
+    def multiply(group, after, weights, resident=True):
         own = [a for k in group for a in (mine[k], peers[k])]
         other = [lax.ppermute(a, "sub", swap) for a in own]
-        result, crossing, *rest = run_expert(where, after, own + other, held, resident)
-        held, resident = (held, True) if resident else (rest, True)
-        crossed = lax.ppermute(crossing, "sub", swap)
-        after = []
-        for i, k in reversed(list(enumerate(group))):
-            at = slice(i * rows, (i + 1) * rows)
-            to_peer = (result[1, at] + crossed[1, at].astype(jnp.float32)).astype(jnp.bfloat16)
-            part = result[0, at] + crossed[0, at].astype(jnp.float32)
-            part = part + lax.ppermute(to_peer, "tp", swap).astype(jnp.float32)
-            after.append(to_peer)
-            if k:
-                part = lax.ppermute(part.astype(jnp.bfloat16), "ep", ahead(-k)).astype(jnp.float32)
-            total = part if total is None else total + part
+        return run_expert(where, after, own + other, weights, resident)
+
+    result, crossing, *weights = multiply((0,), [], [w_gate[0], w_up[0], w_down[0]], False)
+    here = result, lax.ppermute(crossing, "sub", swap)
+    peers |= {k: lax.ppermute(mine[k], "tp", swap) for k in (far, *second)}
+    peers[far] = tie(peers[far], crossing, mine[second[0]])
+    result, crossing = multiply((far,), [mine[k] for k in second], weights)
+    crossing = tie(crossing, peers[second[0]])
+    later = result, lax.ppermute(crossing, "sub", swap)
+    to_peer = add(1, 0, rows, *later)
+    arrived = lax.ppermute(to_peer, "tp", swap)
+    result, crossing = multiply(second, [to_peer], weights)
+    crossing = tie(crossing, arrived)
+    sums = [lax.ppermute(add(0, 0, rows, *later, arrived), "ep", ahead(-far))]
+    crossed = lax.ppermute(crossing, "sub", swap)
+    to_peer = [add(1, i, rows, result, crossed) for i in range(len(second))]
+    arrived = [lax.ppermute(a, "tp", swap) for a in to_peer]
+    sums += [
+        lax.ppermute(add(0, i, rows, result, crossed, arrived[i]), "ep", ahead(-k)) for i, k in enumerate(second)
+    ]
+    last = lax.ppermute(tie(add(1, 0, rows, *here), *to_peer), "tp", swap)
+    total = here[0][0] + here[1][0].astype(jnp.float32)
+    for a in (last, *sums):
+        total = total + a.astype(jnp.float32)
     return total.astype(jnp.bfloat16)
 
 
@@ -198,7 +279,7 @@
         P(("ep", "sub"), "tp", None),
     )
     out_specs = P(("grp", "ep", "sub"), "tp")
-    small = mesh.shape["tp"] == 2 and mesh.shape["sub"] == 2 and mesh.shape["ep"] <= 4
+    small = mesh.shape["tp"] == 2 and mesh.shape["sub"] == 2 and mesh.shape["ep"] == 4
     return jax.shard_map(
         by_rows if small else by_slots, mesh=mesh, in_specs=in_specs, out_specs=out_specs, check_vma=False
     )

time: 104 us -> 85.4 us (0.82)
  waiting for transfers between devices: 59.1 us -> 30.2 us
  starting transfers between devices: 25.8 us -> 34.9 us
  Pallas kernels: 15.1 us -> 18.5 us
  other arithmetic: 3.9 us -> 0.99 us
    ppermute x19 -> x21, waiting for transfers between devices: 47.2 us -> 22.3 us  [the longest x3 8.37 us: by_rows(): peers |= {k: lax.ppermute(mine[k], 'tp', swap) for k in (far, *second)}]
    ppermute x19 -> x21, starting transfers between devices: 11.7 us -> 28.4 us  [the longest x2 11.2 us: by_rows(): lax.ppermute(add(0, i, rows, result, crossed, arrived[i]), 'ep', ahead(-k))]
    ppermute x3, starting transfers between devices: 13.9 us -> 6.44 us  [by_rows(): lax.ppermute(packed, 'ep', ahead(k))]
    ppermute x3, waiting for transfers between devices: 11.4 us -> 5.69 us  [by_rows(): lax.ppermute(packed, 'ep', ahead(k))]
    pallas_call x2 -> x3, Pallas kernels: 15.1 us -> 17 us  [run_expert(): pl.pallas_call(functools.partial(expert_kernel, count, len(after), reside...]
    ppermute x2 -> x1, waiting for transfers between devices: 0.48 us -> 2.15 us  [by_rows(): crossed = lax.ppermute(crossing, 'sub', swap)]
    pallas_call x0 -> x12, Pallas kernels: none -> 1.5 us  [the longest x1 1.01 us: pack(): pl.pallas_call(pack_kernel, out_shape=pltpu.VMEM((tokens.shape[0], tokens...]
    convert_element_type x5 -> x0, other arithmetic: 1.17 us -> none  [the longest x1 0.66 us: by_rows(): gate_values.astype(jnp.float32)[:, :, None]]
  transfers between devices with their start and end apart: 24 -> 25, of which waited for: 10 -> 9; matrix products, arithmetic and copies ran while one was open for 1% -> 0% of each run, Pallas kernels for 0% -> 21%
where the time goes in v3:
time: 85.4 us; the launch traced here: 84.7 us
  starting transfers between devices  34.9 us (41%)
  waiting for transfers between devices  30.2 us (35%)
  Pallas kernels  18.5 us (22%)
  other arithmetic  0.99 us (1%)
    pallas_call x3, Pallas kernels, run_expert(): pl.pallas_call(functools.partial(expert_kernel, count, len(after), reside...  17 us
    ppermute x2, starting transfers between devices, by_rows(): lax.ppermute(add(0, i, rows, result, crossed, arrived[i]), 'ep', ahead(-k))  11.2 us
    ppermute x3, waiting for transfers between devices, by_rows(): peers |= {k: lax.ppermute(mine[k], 'tp', swap) for k in (far, *second)}  8.37 us
    ppermute x2, waiting for transfers between devices, by_rows(): lax.ppermute(add(0, i, rows, result, crossed, arrived[i]), 'ep', ahead(-k))  7.91 us
    ppermute x3, starting transfers between devices, by_rows(): lax.ppermute(packed, 'ep', ahead(k))  6.44 us
    ppermute x3, waiting for transfers between devices, by_rows(): lax.ppermute(packed, 'ep', ahead(k))  5.69 us
    ppermute x1, starting transfers between devices, by_rows(): sums = [lax.ppermute(add(0, 0, rows, *later, arrived), 'ep', ahead(-far))]  5.01 us
    ppermute x1, waiting for transfers between devices, by_rows(): peers = {0: lax.ppermute(packed, 'tp', swap)}  4.06 us
  transfers between devices with their start and end apart: 25, of which 9 were waited for; matrix products, arithmetic and copies ran while one was open for 0% of the time, Pallas kernels for 21%

profile of v3, /device:TPU:0, one launch (start us, length us, event | category | flops | bytes accessed | tf_op | source)
XLA Modules:
  0.0 84.7 jit_solution(3142865570324961451)
XLA Ops:
  0.0 1.0 %shard_map.64.refs_0_ = bf16[64,2176]{1,0:T(8,128)(2,1)S(1)} custom-call(bf16[64,2048]{1,0:T(8,128)(2,1)} %tokens_ref.1, s32[2,64]{1,0:T(2,128)} %bitcast.20, bf16[2,64]{1,0:T(2,128)(2,1)} %bitcast.21), custom_call_target="tpu_custom_call" | custom-call | tf_op jit(solution)/shard_map/pallas_call | solution.py:81
  1.0 3.0 %collective-permute-start = (bf16[64,2176]{1,0:T(8,128)(2,1)S(1)}, bf16[64,2176]{1,0:T(8,128)(2,1)S(1)}, u32[]{:S(2)}, u32[]{:S(2)}) collective-permute-start(bf16[64,2176]{1,0:T(8,128)(2,1)S(1)} %shard_map.64.refs_0_), channel_id=1, source_target_pairs={{0,2},{2,0},{1,3},{3,1},{4,6},{6,4},{5,7},{7,5},{8,10},{10,8},{9,1... | collective-permute-start | bytes 835592 | tf_op jit(solution)/shard_map/ppermute | solution.py:240
  4.0 2.6 %collective-permute-start.6 = (bf16[64,2176]{1,0:T(8,128)(2,1)S(1)}, bf16[64,2176]{1,0:T(8,128)(2,1)S(1)}, u32[]{:S(2)}, u32[]{:S(2)}) collective-permute-start(bf16[64,2176]{1,0:T(8,128)(2,1)S(1)} %shard_map.64.refs_0_), channel_id=1, source_target_pairs={{0,8},{4,12},{8,0},{12,4},{1,9},{5,13},{9,1},{13,5},{2,10},{6,14},... | collective-permute-start | bytes 835592 | tf_op jit(solution)/shard_map/ppermute | solution.py:238
  6.6 4.1 %collective-permute-done.refs_1_ = bf16[64,2176]{1,0:T(8,128)(2,1)S(1)} collective-permute-done((bf16[64,2176]{1,0:T(8,128)(2,1)S(1)}, bf16[64,2176]{1,0:T(8,128)(2,1)S(1)}, u32[]{:S(2)}, u32[]{:S(2)}) %collective-permute-start) | collective-permute-done | bytes 278560 | tf_op jit(solution)/shard_map/ppermute | solution.py:240
  10.7 3.9 %collective-permute-start.5 = (bf16[64,2176]{1,0:T(8,128)(2,1)S(1)}, bf16[64,2176]{1,0:T(8,128)(2,1)S(1)}, u32[]{:S(2)}, u32[]{:S(2)}) collective-permute-start(bf16[64,2176]{1,0:T(8,128)(2,1)S(1)} %shard_map.64.refs_0_), channel_id=1, source_target_pairs={{0,12},{4,0},{8,4},{12,8},{1,13},{5,1},{9,5},{13,9},{2,14},{6,2},{... | collective-permute-start | bytes 835592 | tf_op jit(solution)/shard_map/ppermute | solution.py:238
  14.5 5.7 %collective-permute-done.6.refs_2_ = bf16[64,2176]{1,0:T(8,128)(2,1)S(1)} collective-permute-done((bf16[64,2176]{1,0:T(8,128)(2,1)S(1)}, bf16[64,2176]{1,0:T(8,128)(2,1)S(1)}, u32[]{:S(2)}, u32[]{:S(2)}) %collective-permute-start.6) | collective-permute-done | bytes 278560 | tf_op jit(solution)/shard_map/ppermute | solution.py:238
  20.8 7.7 %shard_map.65 = (f32[2,64,2048]{2,1,0:T(8,128)S(1)}, bf16[2,64,2048]{2,1,0:T(8,128)(2,1)S(1)}, bf16[4096,768]{1,0:T(8,128)(2,1)S(1)}, bf16[4096,768]{1,0:T(8,128)(2,1)S(1)}, bf16[768,4096]{1,0:T(8,128)(2,1)S(1)}) custom-call(s32[2]{0:T(128)S(1)} %pad_add_fusion.where_ref, bf16[64,2176]{1,0:T(8,128)(2,1)S(1)} %shard_map.64.refs_0_, ...), custom_call_target="tpu_custom_call" | custom-call | flops 2415919104 | bytes 18874368 | tf_op jit(solution)/shard_map/pallas_call | solution.py:164
  29.1 1.6 %collective-permute-start.10 = (bf16[64,2176]{1,0:T(8,128)(2,1)S(1)}, bf16[64,2176]{1,0:T(8,128)(2,1)S(1)}, u32[]{:S(2)}, u32[]{:S(2)}) collective-permute-start(bf16[64,2176]{1,0:T(8,128)(2,1)S(1)} %collective-permute-done.4.refs_2_.refs_0_.refs_1_), channel_id=1, source_target_pairs={{0,2},{2,0},{1,3},{3,1},{4,6},{6,4},{5,7},{7,5},{8,10},{10,8},{9,1... | collective-permute-start | bytes 835592 | tf_op jit(solution)/shard_map/ppermute | solution.py:249
  30.7 0.8 collective-permute-start.12
  31.4 3.4 %shard_map.68 = (f32[2,64,2048]{2,1,0:T(8,128)S(1)}, bf16[2,64,2048]{2,1,0:T(8,128)(2,1)S(1)}) custom-call(s32[2]{0:T(128)S(1)} %pad_add_fusion.where_ref, bf16[64,2176]{1,0:T(8,128)(2,1)S(1)} %collective-permute-done.4.refs_2_.refs_0_.refs_1_, bf16[64,2176]{1,0:T(8,128)(2,1)S(1)} %collective-permute-done.5.refs_1_.refs_3_, ...), custom_call_target="tpu_custom_call" | custom-call | flops 2415919104 | bytes 1024 | tf_op jit(solution)/shard_map/pallas_call | solution.py:164
  34.8 3.8 %collective-permute-done.10.refs_1_.refs_2_ = bf16[64,2176]{1,0:T(8,128)(2,1)S(1)} collective-permute-done((bf16[64,2176]{1,0:T(8,128)(2,1)S(1)}, bf16[64,2176]{1,0:T(8,128)(2,1)S(1)}, u32[]{:S(2)}, u32[]{:S(2)}) %collective-permute-start.10) | collective-permute-done | bytes 278560 | tf_op jit(solution)/shard_map/ppermute | solution.py:249
  39.1 4.6 %collective-permute-done.12.refs_4_ = bf16[64,2176]{1,0:T(8,128)(2,1)S(1)} collective-permute-done((bf16[64,2176]{1,0:T(8,128)(2,1)S(1)}, bf16[64,2176]{1,0:T(8,128)(2,1)S(1)}, u32[]{:S(2)}, u32[]{:S(2)}) %collective-permute-start.12) | collective-permute-done | bytes 278560 | tf_op jit(solution)/shard_map/ppermute | solution.py:249
  44.2 1.6 %collective-permute-start.17 = (bf16[64,2048]{1,0:T(8,128)(2,1)S(1)}, bf16[64,2048]{1,0:T(8,128)(2,1)S(1)}, u32[]{:S(2)}, u32[]{:S(2)}) collective-permute-start(bf16[64,2048]{1,0:T(8,128)(2,1)S(1)} %shard_map.70.refs_0_), channel_id=1, source_target_pairs={{0,2},{2,0},{1,3},{3,1},{4,6},{6,4},{5,7},{7,5},{8,10},{10,8},{9,1... | collective-permute-start | bytes 786440 | tf_op jit(solution)/shard_map/ppermute | solution.py:255
  45.9 5.9 %shard_map.71 = (f32[2,128,2048]{2,1,0:T(8,128)S(1)}, bf16[2,128,2048]{2,1,0:T(8,128)(2,1)S(1)}) custom-call(s32[2]{0:T(128)S(1)} %pad_add_fusion.where_ref, bf16[64,2048]{1,0:T(8,128)(2,1)S(1)} %shard_map.70.refs_0_, bf16[64,2176]{1,0:T(8,128)(2,1)S(1)} %collective-permute-done.4.refs_2_.refs_0_.refs_1_, ...), custom_call_target="tpu_custom_call" | custom-call | flops 4831838208 | bytes 1024 | tf_op jit(solution)/shard_map/pallas_call | solution.py:164
  51.9 0.7 collective-permute-done.17.refs_1_.refs_0_
  53.0 2.1 %collective-permute-done.18.refs_1_.refs_2_ = bf16[2,128,2048]{2,1,0:T(8,128)(2,1)S(1)} collective-permute-done((bf16[2,128,2048]{2,1,0:T(8,128)(2,1)S(1)}, bf16[2,128,2048]{2,1,0:T(8,128)(2,1)S(1)}, u32[]{:S(2)}, u32[]{:S(2)}) %collective-permute-start.18) | collective-permute-done | bytes 1048608 | tf_op jit(solution)/shard_map/ppermute | solution.py:259
  55.2 1.6 %collective-permute-start.21 = (bf16[64,2048]{1,0:T(8,128)(2,1)S(1)}, bf16[64,2048]{1,0:T(8,128)(2,1)S(1)}, u32[]{:S(2)}, u32[]{:S(2)}) collective-permute-start(bf16[64,2048]{1,0:T(8,128)(2,1)S(1)} %shard_map.73.refs_1_), channel_id=1, source_target_pairs={{0,2},{2,0},{1,3},{3,1},{4,6},{6,4},{5,7},{7,5},{8,10},{10,8},{9,1... | collective-permute-start | bytes 786440 | tf_op jit(solution)/shard_map/ppermute | solution.py:261
  57.6 5.0 %collective-permute-start.20 = (bf16[64,2048]{1,0:T(8,128)(2,1)S(1)}, bf16[64,2048]{1,0:T(8,128)(2,1)S(1)}, u32[]{:S(2)}, u32[]{:S(2)}) collective-permute-start(bf16[64,2048]{1,0:T(8,128)(2,1)S(1)} %shard_map.76), channel_id=1, source_target_pairs={{0,8},{4,12},{8,0},{12,4},{1,9},{5,13},{9,1},{13,5},{2,10},{6,14},... | collective-permute-start | bytes 786440 | tf_op jit(solution)/shard_map/ppermute | solution.py:258
  63.2 1.3 %collective-permute-done.21.refs_0_ = bf16[64,2048]{1,0:T(8,128)(2,1)S(1)} collective-permute-done((bf16[64,2048]{1,0:T(8,128)(2,1)S(1)}, bf16[64,2048]{1,0:T(8,128)(2,1)S(1)}, u32[]{:S(2)}, u32[]{:S(2)}) %collective-permute-start.21) | collective-permute-done | bytes 262176 | tf_op jit(solution)/shard_map/ppermute | solution.py:261
  64.6 8.5 %collective-permute-start.22 = (bf16[64,2048]{1,0:T(8,128)(2,1)S(1)}, bf16[64,2048]{1,0:T(8,128)(2,1)S(1)}, u32[]{:S(2)}, u32[]{:S(2)}) collective-permute-start(bf16[64,2048]{1,0:T(8,128)(2,1)S(1)} %shard_map.77), channel_id=1, source_target_pairs={{0,12},{4,0},{8,4},{12,8},{1,13},{5,1},{9,5},{13,9},{2,14},{6,2},{... | collective-permute-start | bytes 786440 | tf_op jit(solution)/shard_map/ppermute | solution.py:263
  73.2 2.7 %collective-permute-start.24 = (bf16[64,2048]{1,0:T(8,128)(2,1)S(1)}, bf16[64,2048]{1,0:T(8,128)(2,1)S(1)}, u32[]{:S(2)}, u32[]{:S(2)}) collective-permute-start(bf16[64,2048]{1,0:T(8,128)(2,1)S(1)} %shard_map.78), channel_id=1, source_target_pairs={{0,4},{4,8},{8,12},{12,0},{1,5},{5,9},{9,13},{13,1},{2,6},{6,10},{... | collective-permute-start | bytes 786440 | tf_op jit(solution)/shard_map/ppermute | solution.py:263
  75.9 4.0 %collective-permute-done.22 = bf16[64,2048]{1,0:T(8,128)(2,1)S(1)} collective-permute-done((bf16[64,2048]{1,0:T(8,128)(2,1)S(1)}, bf16[64,2048]{1,0:T(8,128)(2,1)S(1)}, u32[]{:S(2)}, u32[]{:S(2)}) %collective-permute-start.22) | collective-permute-done | bytes 262176 | tf_op jit(solution)/shard_map/ppermute | solution.py:263
  79.8 3.9 %collective-permute-done.24 = bf16[64,2048]{1,0:T(8,128)(2,1)S(1)} collective-permute-done((bf16[64,2048]{1,0:T(8,128)(2,1)S(1)}, bf16[64,2048]{1,0:T(8,128)(2,1)S(1)}, u32[]{:S(2)}, u32[]{:S(2)}) %collective-permute-start.24) | collective-permute-done | bytes 262176 | tf_op jit(solution)/shard_map/ppermute | solution.py:263
  83.8 0.9 %fusion.3 = bf16[64,2048]{1,0:T(8,128)(2,1)} fusion(bf16[64,2048]{1,0:T(8,128)(2,1)S(1)} %collective-permute-done.24, bf16[64,2048]{1,0:T(8,128)(2,1)S(1)} %collective-permute-done.22, bf16[64,2048]{1,0:T(8,128)(2,1)S(1)} %collective-permute-done.20, bf16[64,2048]{1,0:T(8,128)(2,1)S(1)} %collective-permute-done.19, ...), kind=kLoop, calls=%fused_computation.4 | loop fusion | flops 1441792 | bytes 2097152 | tf_op jit(solution)/shard_map/convert_element_type | solution.py:269
  (43 shorter events, 4.2 us)
Async XLA Ops:
  1.0 9.7 %collective-permute-start = (bf16[64,2176]{1,0:T(8,128)(2,1)S(1)}, bf16[64,2176]{1,0:T(8,128)(2,1)S(1)}, u32[]{:S(2)}, u32[]{:S(2)}) collective-permute-start(bf16[64,2176]{1,0:T(8,128)(2,1)S(1)} %shard_map.64.refs_0_), channel_id=1, source_target_pairs={{0,2},{2,0},{1,3},{3,1},{4,6},{6,4},{5,7},{7,5},{8,10},{10,8},{9,1... | collective-permute-start | bytes 835592 | tf_op jit(solution)/shard_map/ppermute | solution.py:240
  4.0 16.2 %collective-permute-start.6 = (bf16[64,2176]{1,0:T(8,128)(2,1)S(1)}, bf16[64,2176]{1,0:T(8,128)(2,1)S(1)}, u32[]{:S(2)}, u32[]{:S(2)}) collective-permute-start(bf16[64,2176]{1,0:T(8,128)(2,1)S(1)} %shard_map.64.refs_0_), channel_id=1, source_target_pairs={{0,8},{4,12},{8,0},{12,4},{1,9},{5,13},{9,1},{13,5},{2,10},{6,14},... | collective-permute-start | bytes 835592 | tf_op jit(solution)/shard_map/ppermute | solution.py:238
  6.6 14.1 %collective-permute-start.1 = (bf16[64,2176]{1,0:T(8,128)(2,1)S(1)}, bf16[64,2176]{1,0:T(8,128)(2,1)S(1)}, u32[]{:S(2)}, u32[]{:S(2)}) collective-permute-start(bf16[64,2176]{1,0:T(8,128)(2,1)S(1)} %shard_map.64.refs_0_), channel_id=1, source_target_pairs={{0,1},{1,0},{2,3},{3,2},{4,5},{5,4},{6,7},{7,6},{8,9},{9,8},{10,11... | collective-permute-start | bytes 835592 | tf_op jit(solution)/shard_map/ppermute | solution.py:244
  10.7 10.1 %collective-permute-start.2 = (bf16[64,2176]{1,0:T(8,128)(2,1)S(1)}, bf16[64,2176]{1,0:T(8,128)(2,1)S(1)}, u32[]{:S(2)}, u32[]{:S(2)}) collective-permute-start(bf16[64,2176]{1,0:T(8,128)(2,1)S(1)} %collective-permute-done.refs_1_), channel_id=1, source_target_pairs={{0,1},{1,0},{2,3},{3,2},{4,5},{5,4},{6,7},{7,6},{8,9},{9,8},{10,11... | collective-permute-start | bytes 835592 | tf_op jit(solution)/shard_map/ppermute | solution.py:244
  10.7 20.0 %collective-permute-start.5 = (bf16[64,2176]{1,0:T(8,128)(2,1)S(1)}, bf16[64,2176]{1,0:T(8,128)(2,1)S(1)}, u32[]{:S(2)}, u32[]{:S(2)}) collective-permute-start(bf16[64,2176]{1,0:T(8,128)(2,1)S(1)} %shard_map.64.refs_0_), channel_id=1, source_target_pairs={{0,12},{4,0},{8,4},{12,8},{1,13},{5,1},{9,5},{13,9},{2,14},{6,2},{... | collective-permute-start | bytes 835592 | tf_op jit(solution)/shard_map/ppermute | solution.py:238
  14.5 14.0 %collective-permute-start.4 = (bf16[64,2176]{1,0:T(8,128)(2,1)S(1)}, bf16[64,2176]{1,0:T(8,128)(2,1)S(1)}, u32[]{:S(2)}, u32[]{:S(2)}) collective-permute-start(bf16[64,2176]{1,0:T(8,128)(2,1)S(1)} %shard_map.64.refs_0_), channel_id=1, source_target_pairs={{0,4},{4,8},{8,12},{12,0},{1,5},{5,9},{9,13},{13,1},{2,6},{6,10},{... | collective-permute-start | bytes 835592 | tf_op jit(solution)/shard_map/ppermute | solution.py:238
  20.2 8.3 %collective-permute-start.7 = (bf16[64,2176]{1,0:T(8,128)(2,1)S(1)}, bf16[64,2176]{1,0:T(8,128)(2,1)S(1)}, u32[]{:S(2)}, u32[]{:S(2)}) collective-permute-start(bf16[64,2176]{1,0:T(8,128)(2,1)S(1)} %collective-permute-done.6.refs_2_), channel_id=1, source_target_pairs={{0,2},{2,0},{1,3},{3,1},{4,6},{6,4},{5,7},{7,5},{8,10},{10,8},{9,1... | collective-permute-start | bytes 835592 | tf_op jit(solution)/shard_map/ppermute | solution.py:249
  20.7 10.7 %collective-permute-start.8 = (bf16[64,2176]{1,0:T(8,128)(2,1)S(1)}, bf16[64,2176]{1,0:T(8,128)(2,1)S(1)}, u32[]{:S(2)}, u32[]{:S(2)}) collective-permute-start(bf16[64,2176]{1,0:T(8,128)(2,1)S(1)} %collective-permute-done.6.refs_2_), channel_id=1, source_target_pairs={{0,1},{1,0},{2,3},{3,2},{4,5},{5,4},{6,7},{7,6},{8,9},{9,8},{10,11... | collective-permute-start | bytes 835592 | tf_op jit(solution)/shard_map/ppermute | solution.py:244
  28.5 2.9 %collective-permute-start.9 = (bf16[64,2176]{1,0:T(8,128)(2,1)S(1)}, bf16[64,2176]{1,0:T(8,128)(2,1)S(1)}, u32[]{:S(2)}, u32[]{:S(2)}) collective-permute-start(bf16[64,2176]{1,0:T(8,128)(2,1)S(1)} %shard_map.67.refs_3_), channel_id=1, source_target_pairs={{0,1},{1,0},{2,3},{3,2},{4,5},{5,4},{6,7},{7,6},{8,9},{9,8},{10,11... | collective-permute-start | bytes 835592 | tf_op jit(solution)/shard_map/ppermute | solution.py:244
  29.1 9.5 %collective-permute-start.10 = (bf16[64,2176]{1,0:T(8,128)(2,1)S(1)}, bf16[64,2176]{1,0:T(8,128)(2,1)S(1)}, u32[]{:S(2)}, u32[]{:S(2)}) collective-permute-start(bf16[64,2176]{1,0:T(8,128)(2,1)S(1)} %collective-permute-done.4.refs_2_.refs_0_.refs_1_), channel_id=1, source_target_pairs={{0,2},{2,0},{1,3},{3,1},{4,6},{6,4},{5,7},{7,5},{8,10},{10,8},{9,1... | collective-permute-start | bytes 835592 | tf_op jit(solution)/shard_map/ppermute | solution.py:249
  30.7 13.0 %collective-permute-start.12 = (bf16[64,2176]{1,0:T(8,128)(2,1)S(1)}, bf16[64,2176]{1,0:T(8,128)(2,1)S(1)}, u32[]{:S(2)}, u32[]{:S(2)}) collective-permute-start(bf16[64,2176]{1,0:T(8,128)(2,1)S(1)} %collective-permute-done.5.refs_1_.refs_3_), channel_id=1, source_target_pairs={{0,2},{2,0},{1,3},{3,1},{4,6},{6,4},{5,7},{7,5},{8,10},{10,8},{9,1... | collective-permute-start | bytes 835592 | tf_op jit(solution)/shard_map/ppermute | solution.py:249
  38.6 5.6 %collective-permute-start.11 = (bf16[2,64,2048]{2,1,0:T(8,128)(2,1)S(1)}, bf16[2,64,2048]{2,1,0:T(8,128)(2,1)S(1)}, u32[]{:S(2)}, u32[]{:S(2)}) collective-permute-start(bf16[2,64,2048]{2,1,0:T(8,128)(2,1)S(1)} %shard_map.69), channel_id=1, source_target_pairs={{0,1},{1,0},{2,3},{3,2},{4,5},{5,4},{6,7},{7,6},{8,9},{9,8},{10,11... | collective-permute-start | bytes 1572872 | tf_op jit(solution)/shard_map/ppermute | solution.py:253
  38.6 7.3 %collective-permute-start.15 = (bf16[64,2176]{1,0:T(8,128)(2,1)S(1)}, bf16[64,2176]{1,0:T(8,128)(2,1)S(1)}, u32[]{:S(2)}, u32[]{:S(2)}) collective-permute-start(bf16[64,2176]{1,0:T(8,128)(2,1)S(1)} %collective-permute-done.5.refs_1_.refs_3_), channel_id=1, source_target_pairs={{0,1},{1,0},{2,3},{3,2},{4,5},{5,4},{6,7},{7,6},{8,9},{9,8},{10,11... | collective-permute-start | bytes 835592 | tf_op jit(solution)/shard_map/ppermute | solution.py:244
  39.1 6.8 %collective-permute-start.13 = (bf16[64,2176]{1,0:T(8,128)(2,1)S(1)}, bf16[64,2176]{1,0:T(8,128)(2,1)S(1)}, u32[]{:S(2)}, u32[]{:S(2)}) collective-permute-start(bf16[64,2176]{1,0:T(8,128)(2,1)S(1)} %collective-permute-done.4.refs_2_.refs_0_.refs_1_), channel_id=1, source_target_pairs={{0,1},{1,0},{2,3},{3,2},{4,5},{5,4},{6,7},{7,6},{8,9},{9,8},{10,11... | collective-permute-start | bytes 835592 | tf_op jit(solution)/shard_map/ppermute | solution.py:244
  43.7 2.2 %collective-permute-start.14 = (bf16[64,2176]{1,0:T(8,128)(2,1)S(1)}, bf16[64,2176]{1,0:T(8,128)(2,1)S(1)}, u32[]{:S(2)}, u32[]{:S(2)}) collective-permute-start(bf16[64,2176]{1,0:T(8,128)(2,1)S(1)} %collective-permute-done.10.refs_1_.refs_2_), channel_id=1, source_target_pairs={{0,1},{1,0},{2,3},{3,2},{4,5},{5,4},{6,7},{7,6},{8,9},{9,8},{10,11... | collective-permute-start | bytes 835592 | tf_op jit(solution)/shard_map/ppermute | solution.py:244
  44.2 8.3 %collective-permute-start.17 = (bf16[64,2048]{1,0:T(8,128)(2,1)S(1)}, bf16[64,2048]{1,0:T(8,128)(2,1)S(1)}, u32[]{:S(2)}, u32[]{:S(2)}) collective-permute-start(bf16[64,2048]{1,0:T(8,128)(2,1)S(1)} %shard_map.70.refs_0_), channel_id=1, source_target_pairs={{0,2},{2,0},{1,3},{3,1},{4,6},{6,4},{5,7},{7,5},{8,10},{10,8},{9,1... | collective-permute-start | bytes 786440 | tf_op jit(solution)/shard_map/ppermute | solution.py:255
  52.5 2.7 %collective-permute-start.18 = (bf16[2,128,2048]{2,1,0:T(8,128)(2,1)S(1)}, bf16[2,128,2048]{2,1,0:T(8,128)(2,1)S(1)}, u32[]{:S(2)}, u32[]{:S(2)}) collective-permute-start(bf16[2,128,2048]{2,1,0:T(8,128)(2,1)S(1)} %shard_map.72), channel_id=1, source_target_pairs={{0,1},{1,0},{2,3},{3,2},{4,5},{5,4},{6,7},{7,6},{8,9},{9,8},{10,11... | collective-permute-start | bytes 3145736 | tf_op jit(solution)/shard_map/ppermute | solution.py:259
  52.5 4.9 %collective-permute-start.3 = (bf16[2,64,2048]{2,1,0:T(8,128)(2,1)S(1)}, bf16[2,64,2048]{2,1,0:T(8,128)(2,1)S(1)}, u32[]{:S(2)}, u32[]{:S(2)}) collective-permute-start(bf16[2,64,2048]{2,1,0:T(8,128)(2,1)S(1)} %get-tuple-element.15.refs_1_), channel_id=1, source_target_pairs={{0,1},{1,0},{2,3},{3,2},{4,5},{5,4},{6,7},{7,6},{8,9},{9,8},{10,11... | collective-permute-start | bytes 1572872 | tf_op jit(solution)/shard_map/ppermute | solution.py:248
  55.2 9.2 %collective-permute-start.21 = (bf16[64,2048]{1,0:T(8,128)(2,1)S(1)}, bf16[64,2048]{1,0:T(8,128)(2,1)S(1)}, u32[]{:S(2)}, u32[]{:S(2)}) collective-permute-start(bf16[64,2048]{1,0:T(8,128)(2,1)S(1)} %shard_map.73.refs_1_), channel_id=1, source_target_pairs={{0,2},{2,0},{1,3},{3,1},{4,6},{6,4},{5,7},{7,5},{8,10},{10,8},{9,1... | collective-permute-start | bytes 786440 | tf_op jit(solution)/shard_map/ppermute | solution.py:261
  56.9 16.1 %collective-permute-start.23 = (bf16[64,2048]{1,0:T(8,128)(2,1)S(1)}, bf16[64,2048]{1,0:T(8,128)(2,1)S(1)}, u32[]{:S(2)}, u32[]{:S(2)}) collective-permute-start(bf16[64,2048]{1,0:T(8,128)(2,1)S(1)} %shard_map.74.refs_2_), channel_id=1, source_target_pairs={{0,2},{2,0},{1,3},{3,1},{4,6},{6,4},{5,7},{7,5},{8,10},{10,8},{9,1... | collective-permute-start | bytes 786440 | tf_op jit(solution)/shard_map/ppermute | solution.py:261
  57.6 18.2 %collective-permute-start.20 = (bf16[64,2048]{1,0:T(8,128)(2,1)S(1)}, bf16[64,2048]{1,0:T(8,128)(2,1)S(1)}, u32[]{:S(2)}, u32[]{:S(2)}) collective-permute-start(bf16[64,2048]{1,0:T(8,128)(2,1)S(1)} %shard_map.76), channel_id=1, source_target_pairs={{0,8},{4,12},{8,0},{12,4},{1,9},{5,13},{9,1},{13,5},{2,10},{6,14},... | collective-permute-start | bytes 786440 | tf_op jit(solution)/shard_map/ppermute | solution.py:258
  62.6 13.2 %collective-permute-start.19 = (bf16[64,2048]{1,0:T(8,128)(2,1)S(1)}, bf16[64,2048]{1,0:T(8,128)(2,1)S(1)}, u32[]{:S(2)}, u32[]{:S(2)}) collective-permute-start(bf16[64,2048]{1,0:T(8,128)(2,1)S(1)} %shard_map.75), channel_id=1, source_target_pairs={{0,2},{2,0},{1,3},{3,1},{4,6},{6,4},{5,7},{7,5},{8,10},{10,8},{9,1... | collective-permute-start | bytes 786440 | tf_op jit(solution)/shard_map/ppermute | solution.py:265
  64.6 15.3 %collective-permute-start.22 = (bf16[64,2048]{1,0:T(8,128)(2,1)S(1)}, bf16[64,2048]{1,0:T(8,128)(2,1)S(1)}, u32[]{:S(2)}, u32[]{:S(2)}) collective-permute-start(bf16[64,2048]{1,0:T(8,128)(2,1)S(1)} %shard_map.77), channel_id=1, source_target_pairs={{0,12},{4,0},{8,4},{12,8},{1,13},{5,1},{9,5},{13,9},{2,14},{6,2},{... | collective-permute-start | bytes 786440 | tf_op jit(solution)/shard_map/ppermute | solution.py:263
  73.2 10.6 %collective-permute-start.24 = (bf16[64,2048]{1,0:T(8,128)(2,1)S(1)}, bf16[64,2048]{1,0:T(8,128)(2,1)S(1)}, u32[]{:S(2)}, u32[]{:S(2)}) collective-permute-start(bf16[64,2048]{1,0:T(8,128)(2,1)S(1)} %shard_map.78), channel_id=1, source_target_pairs={{0,4},{4,8},{8,12},{12,0},{1,5},{5,9},{9,13},{13,1},{2,6},{6,10},{... | collective-permute-start | bytes 786440 | tf_op jit(solution)/shard_map/ppermute | solution.py:263
  (1 other events, 2.2 us)

commit v4 on v3

--- a/solution.py
+++ b/solution.py
@@ -231,11 +231,11 @@
     ep = lax.axis_size("ep")
     rows = tokens.shape[0]
     swap = [(0, 1), (1, 0)]
-    ahead = lambda k: [(i, (i + k) % ep) for i in range(ep)]
+    across = lambda k: [(i, i ^ k) for i in range(ep)]
     far = ep // 2
-    second = tuple(k for k in range(1, ep) if k != far)
+    second = (far + 1, far - 1)
     packed = pack(tokens, expert_ids, gate_values)
-    mine = {k: lax.ppermute(packed, "ep", ahead(k)) if k else packed for k in (far, *second, 0)}
+    mine = {k: lax.ppermute(packed, "ep", across(k)) if k else packed for k in (far, *second, 0)}
     where = jnp.stack([lax.axis_index("tp"), lax.axis_index("ep") * 2 + lax.axis_index("sub")]).astype(jnp.int32)
     peers = {0: lax.ppermute(packed, "tp", swap)}
 
@@ -247,22 +247,22 @@
     result, crossing, *weights = multiply((0,), [], [w_gate[0], w_up[0], w_down[0]], False)
     here = result, lax.ppermute(crossing, "sub", swap)
     peers |= {k: lax.ppermute(mine[k], "tp", swap) for k in (far, *second)}
-    peers[far] = tie(peers[far], crossing, mine[second[0]])
+    peers[far] = tie(peers[far], crossing, mine[second[1]])
     result, crossing = multiply((far,), [mine[k] for k in second], weights)
     crossing = tie(crossing, peers[second[0]])
     later = result, lax.ppermute(crossing, "sub", swap)
     to_peer = add(1, 0, rows, *later)
-    arrived = lax.ppermute(to_peer, "tp", swap)
+    passed = add(0, 0, rows, *later, lax.ppermute(to_peer, "tp", swap))
     result, crossing = multiply(second, [to_peer], weights)
-    crossing = tie(crossing, arrived)
-    sums = [lax.ppermute(add(0, 0, rows, *later, arrived), "ep", ahead(-far))]
-    crossed = lax.ppermute(crossing, "sub", swap)
+    crossed = lax.ppermute(tie(crossing, passed), "sub", swap)
+    passed = lax.ppermute(passed, "ep", across(far ^ second[0]))
     to_peer = [add(1, i, rows, result, crossed) for i in range(len(second))]
     arrived = [lax.ppermute(a, "tp", swap) for a in to_peer]
-    sums += [
-        lax.ppermute(add(0, i, rows, result, crossed, arrived[i]), "ep", ahead(-k)) for i, k in enumerate(second)
+    last = lax.ppermute(tie(add(1, 0, rows, *here), *to_peer), "tp", swap)
+    sums = [
+        lax.ppermute(add(0, 0, rows, result, crossed, arrived[0], passed), "ep", across(second[0])),
+        lax.ppermute(add(0, 1, rows, result, crossed, arrived[1]), "ep", across(second[1])),
     ]
-    last = lax.ppermute(tie(add(1, 0, rows, *here), *to_peer), "tp", swap)
     total = here[0][0] + here[1][0].astype(jnp.float32)
     for a in (last, *sums):
         total = total + a.astype(jnp.float32)

time: 85.4 us -> 82.4 us (0.965)
  starting transfers between devices: 34.9 us -> 22.8 us
  waiting for transfers between devices: 30.2 us -> 39.8 us
    ppermute x8, starting transfers between devices: 24.3 us -> 12.7 us  [the longest x3 6.89 us: by_rows(): lax.ppermute(packed, 'ep', across(k))]
    ppermute x1, waiting for transfers between devices: 0.01 us -> 4.16 us  [by_rows(): last = lax.ppermute(tie(add(1, 0, rows, *here), *to_peer), 'tp', swap)]
    ppermute x2, waiting for transfers between devices: 1.3 us -> 4.77 us  [by_rows(): arrived = [lax.ppermute(a, 'tp', swap) for a in to_peer]]
    ppermute x8, waiting for transfers between devices: 16.4 us -> 17.6 us  [the longest x3 7.41 us: by_rows(): lax.ppermute(packed, 'ep', across(k))]
  transfers between devices with their start and end apart: 25 -> 25, of which waited for: 9 -> 14; matrix products, arithmetic and copies ran while one was open for 0% -> 0% of each run, Pallas kernels for 21% -> 21%
where the time goes in v4:
time: 82.4 us; the launch traced here: 82.2 us
  waiting for transfers between devices  39.8 us (48%)
  starting transfers between devices  22.8 us (28%)
  Pallas kernels  18.6 us (23%)
  other arithmetic  0.95 us (1%)
    pallas_call x3, Pallas kernels, run_expert(): pl.pallas_call(functools.partial(expert_kernel, count, len(after), reside...  17 us
    ppermute x3, waiting for transfers between devices, by_rows(): peers |= {k: lax.ppermute(mine[k], 'tp', swap) for k in (far, *second)}  8.54 us
    ppermute x3, waiting for transfers between devices, by_rows(): lax.ppermute(packed, 'ep', across(k))  7.41 us
    ppermute x3, starting transfers between devices, by_rows(): lax.ppermute(packed, 'ep', across(k))  6.89 us
    ppermute x2, waiting for transfers between devices, by_rows(): arrived = [lax.ppermute(a, 'tp', swap) for a in to_peer]  4.77 us
    ppermute x1, waiting for transfers between devices, by_rows(): last = lax.ppermute(tie(add(1, 0, rows, *here), *to_peer), 'tp', swap)  4.16 us
    ppermute x1, waiting for transfers between devices, by_rows(): peers = {0: lax.ppermute(packed, 'tp', swap)}  4.06 us
    ppermute x1, waiting for transfers between devices, by_rows(): lax.ppermute(add(0, 1, rows, result, crossed, arrived[1]), 'ep', across(s...  3.93 us
  transfers between devices with their start and end apart: 25, of which 14 were waited for; matrix products, arithmetic and copies ran while one was open for 0% of the time, Pallas kernels for 21%

profile of v4, /device:TPU:0, one launch (start us, length us, event | category | flops | bytes accessed | tf_op | source)
XLA Modules:
  0.0 82.2 jit_solution(8447687107356029719)
XLA Ops:
  0.0 1.0 %shard_map.64.refs_0_ = bf16[64,2176]{1,0:T(8,128)(2,1)S(1)} custom-call(bf16[64,2048]{1,0:T(8,128)(2,1)} %tokens_ref.1, s32[2,64]{1,0:T(2,128)} %bitcast.18, bf16[2,64]{1,0:T(2,128)(2,1)} %bitcast.19), custom_call_target="tpu_custom_call" | custom-call | tf_op jit(solution)/shard_map/pallas_call | solution.py:81
  1.0 3.0 %collective-permute-start = (bf16[64,2176]{1,0:T(8,128)(2,1)S(1)}, bf16[64,2176]{1,0:T(8,128)(2,1)S(1)}, u32[]{:S(2)}, u32[]{:S(2)}) collective-permute-start(bf16[64,2176]{1,0:T(8,128)(2,1)S(1)} %shard_map.64.refs_0_), channel_id=1, source_target_pairs={{0,2},{2,0},{1,3},{3,1},{4,6},{6,4},{5,7},{7,5},{8,10},{10,8},{9,1... | collective-permute-start | bytes 835592 | tf_op jit(solution)/shard_map/ppermute | solution.py:240
  4.0 2.6 %collective-permute-start.6 = (bf16[64,2176]{1,0:T(8,128)(2,1)S(1)}, bf16[64,2176]{1,0:T(8,128)(2,1)S(1)}, u32[]{:S(2)}, u32[]{:S(2)}) collective-permute-start(bf16[64,2176]{1,0:T(8,128)(2,1)S(1)} %shard_map.64.refs_0_), channel_id=1, source_target_pairs={{0,8},{4,12},{8,0},{12,4},{1,9},{5,13},{9,1},{13,5},{2,10},{6,14},... | collective-permute-start | bytes 835592 | tf_op jit(solution)/shard_map/ppermute | solution.py:238
  6.6 4.1 %collective-permute-done.refs_1_ = bf16[64,2176]{1,0:T(8,128)(2,1)S(1)} collective-permute-done((bf16[64,2176]{1,0:T(8,128)(2,1)S(1)}, bf16[64,2176]{1,0:T(8,128)(2,1)S(1)}, u32[]{:S(2)}, u32[]{:S(2)}) %collective-permute-start) | collective-permute-done | bytes 278560 | tf_op jit(solution)/shard_map/ppermute | solution.py:240
  10.7 1.8 %collective-permute-start.5 = (bf16[64,2176]{1,0:T(8,128)(2,1)S(1)}, bf16[64,2176]{1,0:T(8,128)(2,1)S(1)}, u32[]{:S(2)}, u32[]{:S(2)}) collective-permute-start(bf16[64,2176]{1,0:T(8,128)(2,1)S(1)} %shard_map.64.refs_0_), channel_id=1, source_target_pairs={{0,4},{4,0},{8,12},{12,8},{1,5},{5,1},{9,13},{13,9},{2,6},{6,2},{1... | collective-permute-start | bytes 835592 | tf_op jit(solution)/shard_map/ppermute | solution.py:238
  12.5 2.5 %collective-permute-start.4 = (bf16[64,2176]{1,0:T(8,128)(2,1)S(1)}, bf16[64,2176]{1,0:T(8,128)(2,1)S(1)}, u32[]{:S(2)}, u32[]{:S(2)}) collective-permute-start(bf16[64,2176]{1,0:T(8,128)(2,1)S(1)} %shard_map.64.refs_0_), channel_id=1, source_target_pairs={{0,12},{4,8},{8,4},{12,0},{1,13},{5,9},{9,5},{13,1},{2,14},{6,10},... | collective-permute-start | bytes 835592 | tf_op jit(solution)/shard_map/ppermute | solution.py:238
  15.0 5.2 %collective-permute-done.6.refs_2_ = bf16[64,2176]{1,0:T(8,128)(2,1)S(1)} collective-permute-done((bf16[64,2176]{1,0:T(8,128)(2,1)S(1)}, bf16[64,2176]{1,0:T(8,128)(2,1)S(1)}, u32[]{:S(2)}, u32[]{:S(2)}) %collective-permute-start.6) | collective-permute-done | bytes 278560 | tf_op jit(solution)/shard_map/ppermute | solution.py:238
  20.8 7.7 %shard_map.65 = (f32[2,64,2048]{2,1,0:T(8,128)S(1)}, bf16[2,64,2048]{2,1,0:T(8,128)(2,1)S(1)}, bf16[4096,768]{1,0:T(8,128)(2,1)S(1)}, bf16[4096,768]{1,0:T(8,128)(2,1)S(1)}, bf16[768,4096]{1,0:T(8,128)(2,1)S(1)}) custom-call(s32[2]{0:T(128)S(1)} %pad_add_fusion.where_ref, bf16[64,2176]{1,0:T(8,128)(2,1)S(1)} %shard_map.64.refs_0_, ...), custom_call_target="tpu_custom_call" | custom-call | flops 2415919104 | bytes 18874368 | tf_op jit(solution)/shard_map/pallas_call | solution.py:164
  28.5 2.2 %collective-permute-done.5.refs_2_.refs_1_.refs_3_ = bf16[64,2176]{1,0:T(8,128)(2,1)S(1)} collective-permute-done((bf16[64,2176]{1,0:T(8,128)(2,1)S(1)}, bf16[64,2176]{1,0:T(8,128)(2,1)S(1)}, u32[]{:S(2)}, u32[]{:S(2)}) %collective-permute-start.5) | collective-permute-done | bytes 278560 | tf_op jit(solution)/shard_map/ppermute | solution.py:238
  31.5 1.3 %collective-permute-start.12 = (bf16[64,2176]{1,0:T(8,128)(2,1)S(1)}, bf16[64,2176]{1,0:T(8,128)(2,1)S(1)}, u32[]{:S(2)}, u32[]{:S(2)}) collective-permute-start(bf16[64,2176]{1,0:T(8,128)(2,1)S(1)} %collective-permute-done.5.refs_2_.refs_1_.refs_3_), channel_id=1, source_target_pairs={{0,2},{2,0},{1,3},{3,1},{4,6},{6,4},{5,7},{7,5},{8,10},{10,8},{9,1... | collective-permute-start | bytes 835592 | tf_op jit(solution)/shard_map/ppermute | solution.py:249
  32.8 3.4 %shard_map.68 = (f32[2,64,2048]{2,1,0:T(8,128)S(1)}, bf16[2,64,2048]{2,1,0:T(8,128)(2,1)S(1)}) custom-call(s32[2]{0:T(128)S(1)} %pad_add_fusion.where_ref, bf16[64,2176]{1,0:T(8,128)(2,1)S(1)} %collective-permute-done.4.refs_0_.refs_1_, bf16[64,2176]{1,0:T(8,128)(2,1)S(1)} %collective-permute-done.5.refs_2_.refs_1_.refs_3_, ...), custom_call_target="tpu_custom_call" | custom-call | flops 2415919104 | bytes 1024 | tf_op jit(solution)/shard_map/pallas_call | solution.py:164
  36.1 4.1 %collective-permute-done.10.refs_1_.refs_2_ = bf16[64,2176]{1,0:T(8,128)(2,1)S(1)} collective-permute-done((bf16[64,2176]{1,0:T(8,128)(2,1)S(1)}, bf16[64,2176]{1,0:T(8,128)(2,1)S(1)}, u32[]{:S(2)}, u32[]{:S(2)}) %collective-permute-start.10) | collective-permute-done | bytes 278560 | tf_op jit(solution)/shard_map/ppermute | solution.py:249
  41.2 4.5 %collective-permute-done.12.refs_4_ = bf16[64,2176]{1,0:T(8,128)(2,1)S(1)} collective-permute-done((bf16[64,2176]{1,0:T(8,128)(2,1)S(1)}, bf16[64,2176]{1,0:T(8,128)(2,1)S(1)}, u32[]{:S(2)}, u32[]{:S(2)}) %collective-permute-start.12) | collective-permute-done | bytes 278560 | tf_op jit(solution)/shard_map/ppermute | solution.py:249
  47.3 5.9 %shard_map.71 = (f32[2,128,2048]{2,1,0:T(8,128)S(1)}, bf16[2,128,2048]{2,1,0:T(8,128)(2,1)S(1)}) custom-call(s32[2]{0:T(128)S(1)} %pad_add_fusion.where_ref, bf16[64,2048]{1,0:T(8,128)(2,1)S(1)} %shard_map.70.refs_0_, bf16[64,2176]{1,0:T(8,128)(2,1)S(1)} %collective-permute-done.4.refs_0_.refs_1_, ...), custom_call_target="tpu_custom_call" | custom-call | flops 4831838208 | bytes 1024 | tf_op jit(solution)/shard_map/pallas_call | solution.py:164
  53.2 1.3 %collective-permute-done.17.refs_0_ = bf16[64,2048]{1,0:T(8,128)(2,1)S(1)} collective-permute-done((bf16[64,2048]{1,0:T(8,128)(2,1)S(1)}, bf16[64,2048]{1,0:T(8,128)(2,1)S(1)}, u32[]{:S(2)}, u32[]{:S(2)}) %collective-permute-start.17) | collective-permute-done | bytes 262176 | tf_op jit(solution)/shard_map/ppermute | solution.py:255
  55.7 1.6 %collective-permute-done.18.refs_1_.refs_3_.refs_2_ = bf16[2,128,2048]{2,1,0:T(8,128)(2,1)S(1)} collective-permute-done((bf16[2,128,2048]{2,1,0:T(8,128)(2,1)S(1)}, bf16[2,128,2048]{2,1,0:T(8,128)(2,1)S(1)}, u32[]{:S(2)}, u32[]{:S(2)}) %collective-permute-start.18) | collective-permute-done | bytes 1048608 | tf_op jit(solution)/shard_map/ppermute | solution.py:257
  58.3 1.3 %collective-permute-start.23 = (bf16[64,2048]{1,0:T(8,128)(2,1)S(1)}, bf16[64,2048]{1,0:T(8,128)(2,1)S(1)}, u32[]{:S(2)}, u32[]{:S(2)}) collective-permute-start(bf16[64,2048]{1,0:T(8,128)(2,1)S(1)} %shard_map.75.refs_2_), channel_id=1, source_target_pairs={{0,2},{2,0},{1,3},{3,1},{4,6},{6,4},{5,7},{7,5},{8,10},{10,8},{9,1... | collective-permute-start | bytes 786440 | tf_op jit(solution)/shard_map/ppermute | solution.py:260
  60.6 3.0 %collective-permute-done.21.refs_1_ = bf16[64,2048]{1,0:T(8,128)(2,1)S(1)} collective-permute-done((bf16[64,2048]{1,0:T(8,128)(2,1)S(1)}, bf16[64,2048]{1,0:T(8,128)(2,1)S(1)}, u32[]{:S(2)}, u32[]{:S(2)}) %collective-permute-start.21) | collective-permute-done | bytes 262176 | tf_op jit(solution)/shard_map/ppermute | solution.py:258
  63.5 3.1 %collective-permute-done.20.refs_0_ = bf16[64,2048]{1,0:T(8,128)(2,1)S(1)} collective-permute-done((bf16[64,2048]{1,0:T(8,128)(2,1)S(1)}, bf16[64,2048]{1,0:T(8,128)(2,1)S(1)}, u32[]{:S(2)}, u32[]{:S(2)}) %collective-permute-start.20) | collective-permute-done | bytes 262176 | tf_op jit(solution)/shard_map/ppermute | solution.py:260
  66.8 3.8 %collective-permute-start.22 = (bf16[64,2048]{1,0:T(8,128)(2,1)S(1)}, bf16[64,2048]{1,0:T(8,128)(2,1)S(1)}, u32[]{:S(2)}, u32[]{:S(2)}) collective-permute-start(bf16[64,2048]{1,0:T(8,128)(2,1)S(1)} %shard_map.77), channel_id=1, source_target_pairs={{0,12},{4,8},{8,4},{12,0},{1,13},{5,9},{9,5},{13,1},{2,14},{6,10},... | collective-permute-start | bytes 786440 | tf_op jit(solution)/shard_map/ppermute | solution.py:263
  70.6 1.6 %collective-permute-done.23.refs_0_ = bf16[64,2048]{1,0:T(8,128)(2,1)S(1)} collective-permute-done((bf16[64,2048]{1,0:T(8,128)(2,1)S(1)}, bf16[64,2048]{1,0:T(8,128)(2,1)S(1)}, u32[]{:S(2)}, u32[]{:S(2)}) %collective-permute-start.23) | collective-permute-done | bytes 262176 | tf_op jit(solution)/shard_map/ppermute | solution.py:260
  72.9 4.2 %collective-permute-done.19 = bf16[64,2048]{1,0:T(8,128)(2,1)S(1)} collective-permute-done((bf16[64,2048]{1,0:T(8,128)(2,1)S(1)}, bf16[64,2048]{1,0:T(8,128)(2,1)S(1)}, u32[]{:S(2)}, u32[]{:S(2)}) %collective-permute-start.19) | collective-permute-done | bytes 262176 | tf_op jit(solution)/shard_map/ppermute | solution.py:261
  77.4 3.9 %collective-permute-done.24 = bf16[64,2048]{1,0:T(8,128)(2,1)S(1)} collective-permute-done((bf16[64,2048]{1,0:T(8,128)(2,1)S(1)}, bf16[64,2048]{1,0:T(8,128)(2,1)S(1)}, u32[]{:S(2)}, u32[]{:S(2)}) %collective-permute-start.24) | collective-permute-done | bytes 262176 | tf_op jit(solution)/shard_map/ppermute | solution.py:264
  81.3 0.9 %fusion.2 = bf16[64,2048]{1,0:T(8,128)(2,1)} fusion(bf16[64,2048]{1,0:T(8,128)(2,1)S(1)} %collective-permute-done.24, bf16[64,2048]{1,0:T(8,128)(2,1)S(1)} %collective-permute-done.22, bf16[64,2048]{1,0:T(8,128)(2,1)S(1)} %collective-permute-done.19, f32[2,64,2048]{2,1,0:T(8,128)S(1)} %get-tuple-element.14.refs_0_, ...), kind=kLoop, calls=%fused_computation.3 | loop fusion | flops 1179648 | bytes 1835008 | tf_op jit(solution)/shard_map/convert_element_type | solution.py:269
  (43 shorter events, 8.1 us)
Async XLA Ops:
  1.0 9.7 %collective-permute-start = (bf16[64,2176]{1,0:T(8,128)(2,1)S(1)}, bf16[64,2176]{1,0:T(8,128)(2,1)S(1)}, u32[]{:S(2)}, u32[]{:S(2)}) collective-permute-start(bf16[64,2176]{1,0:T(8,128)(2,1)S(1)} %shard_map.64.refs_0_), channel_id=1, source_target_pairs={{0,2},{2,0},{1,3},{3,1},{4,6},{6,4},{5,7},{7,5},{8,10},{10,8},{9,1... | collective-permute-start | bytes 835592 | tf_op jit(solution)/shard_map/ppermute | solution.py:240
  4.0 16.2 %collective-permute-start.6 = (bf16[64,2176]{1,0:T(8,128)(2,1)S(1)}, bf16[64,2176]{1,0:T(8,128)(2,1)S(1)}, u32[]{:S(2)}, u32[]{:S(2)}) collective-permute-start(bf16[64,2176]{1,0:T(8,128)(2,1)S(1)} %shard_map.64.refs_0_), channel_id=1, source_target_pairs={{0,8},{4,12},{8,0},{12,4},{1,9},{5,13},{9,1},{13,5},{2,10},{6,14},... | collective-permute-start | bytes 835592 | tf_op jit(solution)/shard_map/ppermute | solution.py:238
  6.6 14.1 %collective-permute-start.1 = (bf16[64,2176]{1,0:T(8,128)(2,1)S(1)}, bf16[64,2176]{1,0:T(8,128)(2,1)S(1)}, u32[]{:S(2)}, u32[]{:S(2)}) collective-permute-start(bf16[64,2176]{1,0:T(8,128)(2,1)S(1)} %shard_map.64.refs_0_), channel_id=1, source_target_pairs={{0,1},{1,0},{2,3},{3,2},{4,5},{5,4},{6,7},{7,6},{8,9},{9,8},{10,11... | collective-permute-start | bytes 835592 | tf_op jit(solution)/shard_map/ppermute | solution.py:244
  10.7 10.1 %collective-permute-start.2 = (bf16[64,2176]{1,0:T(8,128)(2,1)S(1)}, bf16[64,2176]{1,0:T(8,128)(2,1)S(1)}, u32[]{:S(2)}, u32[]{:S(2)}) collective-permute-start(bf16[64,2176]{1,0:T(8,128)(2,1)S(1)} %collective-permute-done.refs_1_), channel_id=1, source_target_pairs={{0,1},{1,0},{2,3},{3,2},{4,5},{5,4},{6,7},{7,6},{8,9},{9,8},{10,11... | collective-permute-start | bytes 835592 | tf_op jit(solution)/shard_map/ppermute | solution.py:244
  10.7 20.0 %collective-permute-start.5 = (bf16[64,2176]{1,0:T(8,128)(2,1)S(1)}, bf16[64,2176]{1,0:T(8,128)(2,1)S(1)}, u32[]{:S(2)}, u32[]{:S(2)}) collective-permute-start(bf16[64,2176]{1,0:T(8,128)(2,1)S(1)} %shard_map.64.refs_0_), channel_id=1, source_target_pairs={{0,4},{4,0},{8,12},{12,8},{1,5},{5,1},{9,13},{13,9},{2,6},{6,2},{1... | collective-permute-start | bytes 835592 | tf_op jit(solution)/shard_map/ppermute | solution.py:238
  12.5 18.2 %collective-permute-start.4 = (bf16[64,2176]{1,0:T(8,128)(2,1)S(1)}, bf16[64,2176]{1,0:T(8,128)(2,1)S(1)}, u32[]{:S(2)}, u32[]{:S(2)}) collective-permute-start(bf16[64,2176]{1,0:T(8,128)(2,1)S(1)} %shard_map.64.refs_0_), channel_id=1, source_target_pairs={{0,12},{4,8},{8,4},{12,0},{1,13},{5,9},{9,5},{13,1},{2,14},{6,10},... | collective-permute-start | bytes 835592 | tf_op jit(solution)/shard_map/ppermute | solution.py:238
  20.2 10.4 %collective-permute-start.7 = (bf16[64,2176]{1,0:T(8,128)(2,1)S(1)}, bf16[64,2176]{1,0:T(8,128)(2,1)S(1)}, u32[]{:S(2)}, u32[]{:S(2)}) collective-permute-start(bf16[64,2176]{1,0:T(8,128)(2,1)S(1)} %collective-permute-done.6.refs_2_), channel_id=1, source_target_pairs={{0,2},{2,0},{1,3},{3,1},{4,6},{6,4},{5,7},{7,5},{8,10},{10,8},{9,1... | collective-permute-start | bytes 835592 | tf_op jit(solution)/shard_map/ppermute | solution.py:249
  20.7 12.0 %collective-permute-start.8 = (bf16[64,2176]{1,0:T(8,128)(2,1)S(1)}, bf16[64,2176]{1,0:T(8,128)(2,1)S(1)}, u32[]{:S(2)}, u32[]{:S(2)}) collective-permute-start(bf16[64,2176]{1,0:T(8,128)(2,1)S(1)} %collective-permute-done.6.refs_2_), channel_id=1, source_target_pairs={{0,1},{1,0},{2,3},{3,2},{4,5},{5,4},{6,7},{7,6},{8,9},{9,8},{10,11... | collective-permute-start | bytes 835592 | tf_op jit(solution)/shard_map/ppermute | solution.py:244
  30.7 2.1 %collective-permute-start.9 = (bf16[64,2176]{1,0:T(8,128)(2,1)S(1)}, bf16[64,2176]{1,0:T(8,128)(2,1)S(1)}, u32[]{:S(2)}, u32[]{:S(2)}) collective-permute-start(bf16[64,2176]{1,0:T(8,128)(2,1)S(1)} %shard_map.67.refs_3_), channel_id=1, source_target_pairs={{0,1},{1,0},{2,3},{3,2},{4,5},{5,4},{6,7},{7,6},{8,9},{9,8},{10,11... | collective-permute-start | bytes 835592 | tf_op jit(solution)/shard_map/ppermute | solution.py:244
  30.7 9.5 %collective-permute-start.10 = (bf16[64,2176]{1,0:T(8,128)(2,1)S(1)}, bf16[64,2176]{1,0:T(8,128)(2,1)S(1)}, u32[]{:S(2)}, u32[]{:S(2)}) collective-permute-start(bf16[64,2176]{1,0:T(8,128)(2,1)S(1)} %collective-permute-done.4.refs_0_.refs_1_), channel_id=1, source_target_pairs={{0,2},{2,0},{1,3},{3,1},{4,6},{6,4},{5,7},{7,5},{8,10},{10,8},{9,1... | collective-permute-start | bytes 835592 | tf_op jit(solution)/shard_map/ppermute | solution.py:249
  31.5 14.2 %collective-permute-start.12 = (bf16[64,2176]{1,0:T(8,128)(2,1)S(1)}, bf16[64,2176]{1,0:T(8,128)(2,1)S(1)}, u32[]{:S(2)}, u32[]{:S(2)}) collective-permute-start(bf16[64,2176]{1,0:T(8,128)(2,1)S(1)} %collective-permute-done.5.refs_2_.refs_1_.refs_3_), channel_id=1, source_target_pairs={{0,2},{2,0},{1,3},{3,1},{4,6},{6,4},{5,7},{7,5},{8,10},{10,8},{9,1... | collective-permute-start | bytes 835592 | tf_op jit(solution)/shard_map/ppermute | solution.py:249
  40.2 5.5 %collective-permute-start.11 = (bf16[2,64,2048]{2,1,0:T(8,128)(2,1)S(1)}, bf16[2,64,2048]{2,1,0:T(8,128)(2,1)S(1)}, u32[]{:S(2)}, u32[]{:S(2)}) collective-permute-start(bf16[2,64,2048]{2,1,0:T(8,128)(2,1)S(1)} %shard_map.69), channel_id=1, source_target_pairs={{0,1},{1,0},{2,3},{3,2},{4,5},{5,4},{6,7},{7,6},{8,9},{9,8},{10,11... | collective-permute-start | bytes 1572872 | tf_op jit(solution)/shard_map/ppermute | solution.py:253
  40.2 6.4 %collective-permute-start.15 = (bf16[64,2176]{1,0:T(8,128)(2,1)S(1)}, bf16[64,2176]{1,0:T(8,128)(2,1)S(1)}, u32[]{:S(2)}, u32[]{:S(2)}) collective-permute-start(bf16[64,2176]{1,0:T(8,128)(2,1)S(1)} %collective-permute-done.5.refs_2_.refs_1_.refs_3_), channel_id=1, source_target_pairs={{0,1},{1,0},{2,3},{3,2},{4,5},{5,4},{6,7},{7,6},{8,9},{9,8},{10,11... | collective-permute-start | bytes 835592 | tf_op jit(solution)/shard_map/ppermute | solution.py:244
  40.7 5.9 %collective-permute-start.13 = (bf16[64,2176]{1,0:T(8,128)(2,1)S(1)}, bf16[64,2176]{1,0:T(8,128)(2,1)S(1)}, u32[]{:S(2)}, u32[]{:S(2)}) collective-permute-start(bf16[64,2176]{1,0:T(8,128)(2,1)S(1)} %collective-permute-done.4.refs_0_.refs_1_), channel_id=1, source_target_pairs={{0,1},{1,0},{2,3},{3,2},{4,5},{5,4},{6,7},{7,6},{8,9},{9,8},{10,11... | collective-permute-start | bytes 835592 | tf_op jit(solution)/shard_map/ppermute | solution.py:244
  40.7 5.9 %collective-permute-start.14 = (bf16[64,2176]{1,0:T(8,128)(2,1)S(1)}, bf16[64,2176]{1,0:T(8,128)(2,1)S(1)}, u32[]{:S(2)}, u32[]{:S(2)}) collective-permute-start(bf16[64,2176]{1,0:T(8,128)(2,1)S(1)} %collective-permute-done.10.refs_1_.refs_2_), channel_id=1, source_target_pairs={{0,1},{1,0},{2,3},{3,2},{4,5},{5,4},{6,7},{7,6},{8,9},{9,8},{10,11... | collective-permute-start | bytes 835592 | tf_op jit(solution)/shard_map/ppermute | solution.py:244
  45.8 8.8 %collective-permute-start.17 = (bf16[64,2048]{1,0:T(8,128)(2,1)S(1)}, bf16[64,2048]{1,0:T(8,128)(2,1)S(1)}, u32[]{:S(2)}, u32[]{:S(2)}) collective-permute-start(bf16[64,2048]{1,0:T(8,128)(2,1)S(1)} %shard_map.70.refs_0_), channel_id=1, source_target_pairs={{0,2},{2,0},{1,3},{3,1},{4,6},{6,4},{5,7},{7,5},{8,10},{10,8},{9,1... | collective-permute-start | bytes 786440 | tf_op jit(solution)/shard_map/ppermute | solution.py:255
  54.6 2.7 %collective-permute-start.18 = (bf16[2,128,2048]{2,1,0:T(8,128)(2,1)S(1)}, bf16[2,128,2048]{2,1,0:T(8,128)(2,1)S(1)}, u32[]{:S(2)}, u32[]{:S(2)}) collective-permute-start(bf16[2,128,2048]{2,1,0:T(8,128)(2,1)S(1)} %shard_map.73), channel_id=1, source_target_pairs={{0,1},{1,0},{2,3},{3,2},{4,5},{5,4},{6,7},{7,6},{8,9},{9,8},{10,11... | collective-permute-start | bytes 3145736 | tf_op jit(solution)/shard_map/ppermute | solution.py:257
  54.7 4.9 %collective-permute-start.3 = (bf16[2,64,2048]{2,1,0:T(8,128)(2,1)S(1)}, bf16[2,64,2048]{2,1,0:T(8,128)(2,1)S(1)}, u32[]{:S(2)}, u32[]{:S(2)}) collective-permute-start(bf16[2,64,2048]{2,1,0:T(8,128)(2,1)S(1)} %get-tuple-element.15.refs_1_), channel_id=1, source_target_pairs={{0,1},{1,0},{2,3},{3,2},{4,5},{5,4},{6,7},{7,6},{8,9},{9,8},{10,11... | collective-permute-start | bytes 1572872 | tf_op jit(solution)/shard_map/ppermute | solution.py:248
  55.2 8.3 %collective-permute-start.21 = (bf16[64,2048]{1,0:T(8,128)(2,1)S(1)}, bf16[64,2048]{1,0:T(8,128)(2,1)S(1)}, u32[]{:S(2)}, u32[]{:S(2)}) collective-permute-start(bf16[64,2048]{1,0:T(8,128)(2,1)S(1)} %shard_map.72.refs_1_), channel_id=1, source_target_pairs={{0,4},{4,0},{8,12},{12,8},{1,5},{5,1},{9,13},{13,9},{2,6},{6,2},{1... | collective-permute-start | bytes 786440 | tf_op jit(solution)/shard_map/ppermute | solution.py:258
  57.4 9.2 %collective-permute-start.20 = (bf16[64,2048]{1,0:T(8,128)(2,1)S(1)}, bf16[64,2048]{1,0:T(8,128)(2,1)S(1)}, u32[]{:S(2)}, u32[]{:S(2)}) collective-permute-start(bf16[64,2048]{1,0:T(8,128)(2,1)S(1)} %shard_map.74.refs_1_), channel_id=1, source_target_pairs={{0,2},{2,0},{1,3},{3,1},{4,6},{6,4},{5,7},{7,5},{8,10},{10,8},{9,1... | collective-permute-start | bytes 786440 | tf_op jit(solution)/shard_map/ppermute | solution.py:260
  58.3 13.9 %collective-permute-start.23 = (bf16[64,2048]{1,0:T(8,128)(2,1)S(1)}, bf16[64,2048]{1,0:T(8,128)(2,1)S(1)}, u32[]{:S(2)}, u32[]{:S(2)}) collective-permute-start(bf16[64,2048]{1,0:T(8,128)(2,1)S(1)} %shard_map.75.refs_2_), channel_id=1, source_target_pairs={{0,2},{2,0},{1,3},{3,1},{4,6},{6,4},{5,7},{7,5},{8,10},{10,8},{9,1... | collective-permute-start | bytes 786440 | tf_op jit(solution)/shard_map/ppermute | solution.py:260
  59.7 17.4 %collective-permute-start.19 = (bf16[64,2048]{1,0:T(8,128)(2,1)S(1)}, bf16[64,2048]{1,0:T(8,128)(2,1)S(1)}, u32[]{:S(2)}, u32[]{:S(2)}) collective-permute-start(bf16[64,2048]{1,0:T(8,128)(2,1)S(1)} %shard_map.76), channel_id=1, source_target_pairs={{0,2},{2,0},{1,3},{3,1},{4,6},{6,4},{5,7},{7,5},{8,10},{10,8},{9,1... | collective-permute-start | bytes 786440 | tf_op jit(solution)/shard_map/ppermute | solution.py:261
  66.8 10.6 %collective-permute-start.22 = (bf16[64,2048]{1,0:T(8,128)(2,1)S(1)}, bf16[64,2048]{1,0:T(8,128)(2,1)S(1)}, u32[]{:S(2)}, u32[]{:S(2)}) collective-permute-start(bf16[64,2048]{1,0:T(8,128)(2,1)S(1)} %shard_map.77), channel_id=1, source_target_pairs={{0,12},{4,8},{8,4},{12,0},{1,13},{5,9},{9,5},{13,1},{2,14},{6,10},... | collective-permute-start | bytes 786440 | tf_op jit(solution)/shard_map/ppermute | solution.py:263
  72.4 9.0 %collective-permute-start.24 = (bf16[64,2048]{1,0:T(8,128)(2,1)S(1)}, bf16[64,2048]{1,0:T(8,128)(2,1)S(1)}, u32[]{:S(2)}, u32[]{:S(2)}) collective-permute-start(bf16[64,2048]{1,0:T(8,128)(2,1)S(1)} %shard_map.78), channel_id=1, source_target_pairs={{0,4},{4,0},{8,12},{12,8},{1,5},{5,1},{9,13},{13,9},{2,6},{6,2},{1... | collective-permute-start | bytes 786440 | tf_op jit(solution)/shard_map/ppermute | solution.py:264
  (1 other events, 1.6 us)

commit v5 on v4

--- a/solution.py
+++ b/solution.py
@@ -247,9 +247,8 @@
     result, crossing, *weights = multiply((0,), [], [w_gate[0], w_up[0], w_down[0]], False)
     here = result, lax.ppermute(crossing, "sub", swap)
     peers |= {k: lax.ppermute(mine[k], "tp", swap) for k in (far, *second)}
-    peers[far] = tie(peers[far], crossing, mine[second[1]])
+    peers[far] = tie(peers[far], crossing, peers[second[1]])
     result, crossing = multiply((far,), [mine[k] for k in second], weights)
-    crossing = tie(crossing, peers[second[0]])
     later = result, lax.ppermute(crossing, "sub", swap)
     to_peer = add(1, 0, rows, *later)
     passed = add(0, 0, rows, *later, lax.ppermute(to_peer, "tp", swap))

time: 82.4 us -> 80.5 us (0.977)
  waiting for transfers between devices: 39.8 us -> 34.3 us
  starting transfers between devices: 22.8 us -> 26.4 us
    ppermute x3, waiting for transfers between devices: 8.54 us -> 2.45 us  [by_rows(): peers |= {k: lax.ppermute(mine[k], 'tp', swap) for k in (far, *second)}]
    ppermute x3, waiting for transfers between devices: 7.41 us -> 11.7 us  [by_rows(): lax.ppermute(packed, 'ep', across(k))]
    ppermute x1, waiting for transfers between devices: 4.06 us -> 2.49 us  [by_rows(): peers = {0: lax.ppermute(packed, 'tp', swap)}]
    ppermute x3, starting transfers between devices: 6.89 us -> 8.02 us  [by_rows(): lax.ppermute(packed, 'ep', across(k))]
    ppermute x1, starting transfers between devices: 0.83 us -> 1.81 us  [by_rows(): passed = add(0, 0, rows, *later, lax.ppermute(to_peer, 'tp', swap))]
    ppermute x1, starting transfers between devices: 0.83 us -> 1.81 us  [by_rows(): last = lax.ppermute(tie(add(1, 0, rows, *here), *to_peer), 'tp', swap)]
    ppermute x1, waiting for transfers between devices: 2.95 us -> 1.98 us  [by_rows(): passed = lax.ppermute(passed, 'ep', across(far ^ second[0]))]
  transfers between devices with their start and end apart: 25 -> 25, of which waited for: 14 -> 11; matrix products, arithmetic and copies ran while one was open for 0% -> 0% of each run, Pallas kernels for 21% -> 22%
where the time goes in v5:
time: 80.5 us; the launch traced here: 80.4 us
  waiting for transfers between devices  34.3 us (43%)
  starting transfers between devices  26.4 us (33%)
  Pallas kernels  18.6 us (23%)
  other arithmetic  0.95 us (1%)
    pallas_call x3, Pallas kernels, run_expert(): pl.pallas_call(functools.partial(expert_kernel, count, len(after), reside...  17 us
    ppermute x3, waiting for transfers between devices, by_rows(): lax.ppermute(packed, 'ep', across(k))  11.7 us
    ppermute x3, starting transfers between devices, by_rows(): lax.ppermute(packed, 'ep', across(k))  8.02 us
    ppermute x2, waiting for transfers between devices, by_rows(): arrived = [lax.ppermute(a, 'tp', swap) for a in to_peer]  5.08 us
    ppermute x1, waiting for transfers between devices, by_rows(): last = lax.ppermute(tie(add(1, 0, rows, *here), *to_peer), 'tp', swap)  4.02 us
    ppermute x1, waiting for transfers between devices, by_rows(): lax.ppermute(add(0, 1, rows, result, crossed, arrived[1]), 'ep', across(s...  4.01 us
    ppermute x1, starting transfers between devices, by_rows(): lax.ppermute(add(0, 0, rows, result, crossed, arrived[0], passed), 'ep',...  3.53 us
    ppermute x1, starting transfers between devices, by_rows(): peers = {0: lax.ppermute(packed, 'tp', swap)}  3 us
  transfers between devices with their start and end apart: 25, of which 11 were waited for; matrix products, arithmetic and copies ran while one was open for 0% of the time, Pallas kernels for 22%

profile of v5, /device:TPU:0, one launch (start us, length us, event | category | flops | bytes accessed | tf_op | source)
XLA Modules:
  0.0 80.4 jit_solution(14698689406746953166)
XLA Ops:
  0.0 1.0 %shard_map.64.refs_0_ = bf16[64,2176]{1,0:T(8,128)(2,1)S(1)} custom-call(bf16[64,2048]{1,0:T(8,128)(2,1)} %tokens_ref.1, s32[2,64]{1,0:T(2,128)} %bitcast.18, bf16[2,64]{1,0:T(2,128)(2,1)} %bitcast.19), custom_call_target="tpu_custom_call" | custom-call | tf_op jit(solution)/shard_map/pallas_call | solution.py:81
  1.0 3.0 %collective-permute-start = (bf16[64,2176]{1,0:T(8,128)(2,1)S(1)}, bf16[64,2176]{1,0:T(8,128)(2,1)S(1)}, u32[]{:S(2)}, u32[]{:S(2)}) collective-permute-start(bf16[64,2176]{1,0:T(8,128)(2,1)S(1)} %shard_map.64.refs_0_), channel_id=1, source_target_pairs={{0,2},{2,0},{1,3},{3,1},{4,6},{6,4},{5,7},{7,5},{8,10},{10,8},{9,1... | collective-permute-start | bytes 835592 | tf_op jit(solution)/shard_map/ppermute | solution.py:240
  4.0 1.6 %collective-permute-start.5 = (bf16[64,2176]{1,0:T(8,128)(2,1)S(1)}, bf16[64,2176]{1,0:T(8,128)(2,1)S(1)}, u32[]{:S(2)}, u32[]{:S(2)}) collective-permute-start(bf16[64,2176]{1,0:T(8,128)(2,1)S(1)} %shard_map.64.refs_0_), channel_id=1, source_target_pairs={{0,4},{4,0},{8,12},{12,8},{1,5},{5,1},{9,13},{13,9},{2,6},{6,2},{1... | collective-permute-start | bytes 835592 | tf_op jit(solution)/shard_map/ppermute | solution.py:238
  5.6 2.6 %collective-permute-start.6 = (bf16[64,2176]{1,0:T(8,128)(2,1)S(1)}, bf16[64,2176]{1,0:T(8,128)(2,1)S(1)}, u32[]{:S(2)}, u32[]{:S(2)}) collective-permute-start(bf16[64,2176]{1,0:T(8,128)(2,1)S(1)} %shard_map.64.refs_0_), channel_id=1, source_target_pairs={{0,8},{4,12},{8,0},{12,4},{1,9},{5,13},{9,1},{13,5},{2,10},{6,14},... | collective-permute-start | bytes 835592 | tf_op jit(solution)/shard_map/ppermute | solution.py:238
  8.2 2.5 %collective-permute-done.refs_1_ = bf16[64,2176]{1,0:T(8,128)(2,1)S(1)} collective-permute-done((bf16[64,2176]{1,0:T(8,128)(2,1)S(1)}, bf16[64,2176]{1,0:T(8,128)(2,1)S(1)}, u32[]{:S(2)}, u32[]{:S(2)}) %collective-permute-start) | collective-permute-done | bytes 278560 | tf_op jit(solution)/shard_map/ppermute | solution.py:240
  10.7 3.9 %collective-permute-start.4 = (bf16[64,2176]{1,0:T(8,128)(2,1)S(1)}, bf16[64,2176]{1,0:T(8,128)(2,1)S(1)}, u32[]{:S(2)}, u32[]{:S(2)}) collective-permute-start(bf16[64,2176]{1,0:T(8,128)(2,1)S(1)} %shard_map.64.refs_0_), channel_id=1, source_target_pairs={{0,12},{4,8},{8,4},{12,0},{1,13},{5,9},{9,5},{13,1},{2,14},{6,10},... | collective-permute-start | bytes 835592 | tf_op jit(solution)/shard_map/ppermute | solution.py:238
  14.5 3.3 %collective-permute-done.5.refs_1_.refs_3_ = bf16[64,2176]{1,0:T(8,128)(2,1)S(1)} collective-permute-done((bf16[64,2176]{1,0:T(8,128)(2,1)S(1)}, bf16[64,2176]{1,0:T(8,128)(2,1)S(1)}, u32[]{:S(2)}, u32[]{:S(2)}) %collective-permute-start.5) | collective-permute-done | bytes 278560 | tf_op jit(solution)/shard_map/ppermute | solution.py:238
  18.4 8.4 %collective-permute-done.6.refs_2_ = bf16[64,2176]{1,0:T(8,128)(2,1)S(1)} collective-permute-done((bf16[64,2176]{1,0:T(8,128)(2,1)S(1)}, bf16[64,2176]{1,0:T(8,128)(2,1)S(1)}, u32[]{:S(2)}, u32[]{:S(2)}) %collective-permute-start.6) | collective-permute-done | bytes 278560 | tf_op jit(solution)/shard_map/ppermute | solution.py:238
  27.0 7.7 %shard_map.65 = (f32[2,64,2048]{2,1,0:T(8,128)S(1)}, bf16[2,64,2048]{2,1,0:T(8,128)(2,1)S(1)}, bf16[4096,768]{1,0:T(8,128)(2,1)S(1)}, bf16[4096,768]{1,0:T(8,128)(2,1)S(1)}, bf16[768,4096]{1,0:T(8,128)(2,1)S(1)}) custom-call(s32[2]{0:T(128)S(1)} %pad_add_fusion.where_ref, bf16[64,2176]{1,0:T(8,128)(2,1)S(1)} %shard_map.64.refs_0_, ...), custom_call_target="tpu_custom_call" | custom-call | flops 2415919104 | bytes 18874368 | tf_op jit(solution)/shard_map/pallas_call | solution.py:164
  35.3 1.9 %collective-permute-start.12 = (bf16[64,2176]{1,0:T(8,128)(2,1)S(1)}, bf16[64,2176]{1,0:T(8,128)(2,1)S(1)}, u32[]{:S(2)}, u32[]{:S(2)}) collective-permute-start(bf16[64,2176]{1,0:T(8,128)(2,1)S(1)} %collective-permute-done.4.refs_0_.refs_1_), channel_id=1, source_target_pairs={{0,2},{2,0},{1,3},{3,1},{4,6},{6,4},{5,7},{7,5},{8,10},{10,8},{9,1... | collective-permute-start | bytes 835592 | tf_op jit(solution)/shard_map/ppermute | solution.py:249
  37.2 3.4 %shard_map.68 = (f32[2,64,2048]{2,1,0:T(8,128)S(1)}, bf16[2,64,2048]{2,1,0:T(8,128)(2,1)S(1)}) custom-call(s32[2]{0:T(128)S(1)} %pad_add_fusion.where_ref, bf16[64,2176]{1,0:T(8,128)(2,1)S(1)} %collective-permute-done.4.refs_0_.refs_1_, bf16[64,2176]{1,0:T(8,128)(2,1)S(1)} %collective-permute-done.5.refs_1_.refs_3_, ...), custom_call_target="tpu_custom_call" | custom-call | flops 2415919104 | bytes 1024 | tf_op jit(solution)/shard_map/pallas_call | solution.py:164
  41.7 2.4 %collective-permute-done.12.refs_2_ = bf16[64,2176]{1,0:T(8,128)(2,1)S(1)} collective-permute-done((bf16[64,2176]{1,0:T(8,128)(2,1)S(1)}, bf16[64,2176]{1,0:T(8,128)(2,1)S(1)}, u32[]{:S(2)}, u32[]{:S(2)}) %collective-permute-start.12) | collective-permute-done | bytes 278560 | tf_op jit(solution)/shard_map/ppermute | solution.py:249
  44.2 1.8 %collective-permute-start.17 = (bf16[64,2048]{1,0:T(8,128)(2,1)S(1)}, bf16[64,2048]{1,0:T(8,128)(2,1)S(1)}, u32[]{:S(2)}, u32[]{:S(2)}) collective-permute-start(bf16[64,2048]{1,0:T(8,128)(2,1)S(1)} %shard_map.69.refs_0_), channel_id=1, source_target_pairs={{0,2},{2,0},{1,3},{3,1},{4,6},{6,4},{5,7},{7,5},{8,10},{10,8},{9,1... | collective-permute-start | bytes 786440 | tf_op jit(solution)/shard_map/ppermute | solution.py:254
  46.0 5.9 %shard_map.70 = (f32[2,128,2048]{2,1,0:T(8,128)S(1)}, bf16[2,128,2048]{2,1,0:T(8,128)(2,1)S(1)}) custom-call(s32[2]{0:T(128)S(1)} %pad_add_fusion.where_ref, bf16[64,2048]{1,0:T(8,128)(2,1)S(1)} %shard_map.69.refs_0_, bf16[64,2176]{1,0:T(8,128)(2,1)S(1)} %collective-permute-done.4.refs_0_.refs_1_, bf16[64,2176]{1,0:T(8,128)(2,1)S(1)} %collective-permute-done.12.refs_2_, ...), custom_call_target="tpu_custom_call" | custom-call | flops 4831838208 | bytes 1024 | tf_op jit(solution)/shard_map/pallas_call | solution.py:164
  51.9 1.0 %collective-permute-done.17.refs_0_ = bf16[64,2048]{1,0:T(8,128)(2,1)S(1)} collective-permute-done((bf16[64,2048]{1,0:T(8,128)(2,1)S(1)}, bf16[64,2048]{1,0:T(8,128)(2,1)S(1)}, u32[]{:S(2)}, u32[]{:S(2)}) %collective-permute-start.17) | collective-permute-done | bytes 262176 | tf_op jit(solution)/shard_map/ppermute | solution.py:254
  54.2 1.5 %collective-permute-done.18.refs_1_.refs_3_.refs_2_ = bf16[2,128,2048]{2,1,0:T(8,128)(2,1)S(1)} collective-permute-done((bf16[2,128,2048]{2,1,0:T(8,128)(2,1)S(1)}, bf16[2,128,2048]{2,1,0:T(8,128)(2,1)S(1)}, u32[]{:S(2)}, u32[]{:S(2)}) %collective-permute-start.18) | collective-permute-done | bytes 1048608 | tf_op jit(solution)/shard_map/ppermute | solution.py:256
  55.8 1.8 %collective-permute-start.20 = (bf16[64,2048]{1,0:T(8,128)(2,1)S(1)}, bf16[64,2048]{1,0:T(8,128)(2,1)S(1)}, u32[]{:S(2)}, u32[]{:S(2)}) collective-permute-start(bf16[64,2048]{1,0:T(8,128)(2,1)S(1)} %shard_map.73.refs_1_), channel_id=1, source_target_pairs={{0,2},{2,0},{1,3},{3,1},{4,6},{6,4},{5,7},{7,5},{8,10},{10,8},{9,1... | collective-permute-start | bytes 786440 | tf_op jit(solution)/shard_map/ppermute | solution.py:259
  58.1 1.8 %collective-permute-start.19 = (bf16[64,2048]{1,0:T(8,128)(2,1)S(1)}, bf16[64,2048]{1,0:T(8,128)(2,1)S(1)}, u32[]{:S(2)}, u32[]{:S(2)}) collective-permute-start(bf16[64,2048]{1,0:T(8,128)(2,1)S(1)} %shard_map.75), channel_id=1, source_target_pairs={{0,2},{2,0},{1,3},{3,1},{4,6},{6,4},{5,7},{7,5},{8,10},{10,8},{9,1... | collective-permute-start | bytes 786440 | tf_op jit(solution)/shard_map/ppermute | solution.py:260
  59.9 2.0 %collective-permute-done.21.refs_1_ = bf16[64,2048]{1,0:T(8,128)(2,1)S(1)} collective-permute-done((bf16[64,2048]{1,0:T(8,128)(2,1)S(1)}, bf16[64,2048]{1,0:T(8,128)(2,1)S(1)}, u32[]{:S(2)}, u32[]{:S(2)}) %collective-permute-start.21) | collective-permute-done | bytes 262176 | tf_op jit(solution)/shard_map/ppermute | solution.py:257
  61.9 3.1 %collective-permute-done.20.refs_0_ = bf16[64,2048]{1,0:T(8,128)(2,1)S(1)} collective-permute-done((bf16[64,2048]{1,0:T(8,128)(2,1)S(1)}, bf16[64,2048]{1,0:T(8,128)(2,1)S(1)}, u32[]{:S(2)}, u32[]{:S(2)}) %collective-permute-start.20) | collective-permute-done | bytes 262176 | tf_op jit(solution)/shard_map/ppermute | solution.py:259
  65.2 3.5 %collective-permute-start.22 = (bf16[64,2048]{1,0:T(8,128)(2,1)S(1)}, bf16[64,2048]{1,0:T(8,128)(2,1)S(1)}, u32[]{:S(2)}, u32[]{:S(2)}) collective-permute-start(bf16[64,2048]{1,0:T(8,128)(2,1)S(1)} %shard_map.76), channel_id=1, source_target_pairs={{0,12},{4,8},{8,4},{12,0},{1,13},{5,9},{9,5},{13,1},{2,14},{6,10},... | collective-permute-start | bytes 786440 | tf_op jit(solution)/shard_map/ppermute | solution.py:262
  68.7 1.9 %collective-permute-done.23.refs_0_ = bf16[64,2048]{1,0:T(8,128)(2,1)S(1)} collective-permute-done((bf16[64,2048]{1,0:T(8,128)(2,1)S(1)}, bf16[64,2048]{1,0:T(8,128)(2,1)S(1)}, u32[]{:S(2)}, u32[]{:S(2)}) %collective-permute-start.23) | collective-permute-done | bytes 262176 | tf_op jit(solution)/shard_map/ppermute | solution.py:259
  71.4 4.0 %collective-permute-done.19 = bf16[64,2048]{1,0:T(8,128)(2,1)S(1)} collective-permute-done((bf16[64,2048]{1,0:T(8,128)(2,1)S(1)}, bf16[64,2048]{1,0:T(8,128)(2,1)S(1)}, u32[]{:S(2)}, u32[]{:S(2)}) %collective-permute-start.19) | collective-permute-done | bytes 262176 | tf_op jit(solution)/shard_map/ppermute | solution.py:260
  75.5 4.0 %collective-permute-done.24 = bf16[64,2048]{1,0:T(8,128)(2,1)S(1)} collective-permute-done((bf16[64,2048]{1,0:T(8,128)(2,1)S(1)}, bf16[64,2048]{1,0:T(8,128)(2,1)S(1)}, u32[]{:S(2)}, u32[]{:S(2)}) %collective-permute-start.24) | collective-permute-done | bytes 262176 | tf_op jit(solution)/shard_map/ppermute | solution.py:263
  (42 shorter events, 6.1 us)
Async XLA Ops:
  1.0 9.7 %collective-permute-start = (bf16[64,2176]{1,0:T(8,128)(2,1)S(1)}, bf16[64,2176]{1,0:T(8,128)(2,1)S(1)}, u32[]{:S(2)}, u32[]{:S(2)}) collective-permute-start(bf16[64,2176]{1,0:T(8,128)(2,1)S(1)} %shard_map.64.refs_0_), channel_id=1, source_target_pairs={{0,2},{2,0},{1,3},{3,1},{4,6},{6,4},{5,7},{7,5},{8,10},{10,8},{9,1... | collective-permute-start | bytes 835592 | tf_op jit(solution)/shard_map/ppermute | solution.py:240
  4.0 13.8 %collective-permute-start.5 = (bf16[64,2176]{1,0:T(8,128)(2,1)S(1)}, bf16[64,2176]{1,0:T(8,128)(2,1)S(1)}, u32[]{:S(2)}, u32[]{:S(2)}) collective-permute-start(bf16[64,2176]{1,0:T(8,128)(2,1)S(1)} %shard_map.64.refs_0_), channel_id=1, source_target_pairs={{0,4},{4,0},{8,12},{12,8},{1,5},{5,1},{9,13},{13,9},{2,6},{6,2},{1... | collective-permute-start | bytes 835592 | tf_op jit(solution)/shard_map/ppermute | solution.py:238
  5.6 21.2 %collective-permute-start.6 = (bf16[64,2176]{1,0:T(8,128)(2,1)S(1)}, bf16[64,2176]{1,0:T(8,128)(2,1)S(1)}, u32[]{:S(2)}, u32[]{:S(2)}) collective-permute-start(bf16[64,2176]{1,0:T(8,128)(2,1)S(1)} %shard_map.64.refs_0_), channel_id=1, source_target_pairs={{0,8},{4,12},{8,0},{12,4},{1,9},{5,13},{9,1},{13,5},{2,10},{6,14},... | collective-permute-start | bytes 835592 | tf_op jit(solution)/shard_map/ppermute | solution.py:238
  8.2 18.8 %collective-permute-start.1 = (bf16[64,2176]{1,0:T(8,128)(2,1)S(1)}, bf16[64,2176]{1,0:T(8,128)(2,1)S(1)}, u32[]{:S(2)}, u32[]{:S(2)}) collective-permute-start(bf16[64,2176]{1,0:T(8,128)(2,1)S(1)} %shard_map.64.refs_0_), channel_id=1, source_target_pairs={{0,1},{1,0},{2,3},{3,2},{4,5},{5,4},{6,7},{7,6},{8,9},{9,8},{10,11... | collective-permute-start | bytes 835592 | tf_op jit(solution)/shard_map/ppermute | solution.py:244
  10.7 16.3 %collective-permute-start.2 = (bf16[64,2176]{1,0:T(8,128)(2,1)S(1)}, bf16[64,2176]{1,0:T(8,128)(2,1)S(1)}, u32[]{:S(2)}, u32[]{:S(2)}) collective-permute-start(bf16[64,2176]{1,0:T(8,128)(2,1)S(1)} %collective-permute-done.refs_1_), channel_id=1, source_target_pairs={{0,1},{1,0},{2,3},{3,2},{4,5},{5,4},{6,7},{7,6},{8,9},{9,8},{10,11... | collective-permute-start | bytes 835592 | tf_op jit(solution)/shard_map/ppermute | solution.py:244
  10.7 24.6 %collective-permute-start.4 = (bf16[64,2176]{1,0:T(8,128)(2,1)S(1)}, bf16[64,2176]{1,0:T(8,128)(2,1)S(1)}, u32[]{:S(2)}, u32[]{:S(2)}) collective-permute-start(bf16[64,2176]{1,0:T(8,128)(2,1)S(1)} %shard_map.64.refs_0_), channel_id=1, source_target_pairs={{0,12},{4,8},{8,4},{12,0},{1,13},{5,9},{9,5},{13,1},{2,14},{6,10},... | collective-permute-start | bytes 835592 | tf_op jit(solution)/shard_map/ppermute | solution.py:238
  17.8 16.9 %collective-permute-start.8 = (bf16[64,2176]{1,0:T(8,128)(2,1)S(1)}, bf16[64,2176]{1,0:T(8,128)(2,1)S(1)}, u32[]{:S(2)}, u32[]{:S(2)}) collective-permute-start(bf16[64,2176]{1,0:T(8,128)(2,1)S(1)} %collective-permute-done.5.refs_1_.refs_3_), channel_id=1, source_target_pairs={{0,2},{2,0},{1,3},{3,1},{4,6},{6,4},{5,7},{7,5},{8,10},{10,8},{9,1... | collective-permute-start | bytes 835592 | tf_op jit(solution)/shard_map/ppermute | solution.py:249
  26.8 8.0 %collective-permute-start.7 = (bf16[64,2176]{1,0:T(8,128)(2,1)S(1)}, bf16[64,2176]{1,0:T(8,128)(2,1)S(1)}, u32[]{:S(2)}, u32[]{:S(2)}) collective-permute-start(bf16[64,2176]{1,0:T(8,128)(2,1)S(1)} %collective-permute-done.6.refs_2_), channel_id=1, source_target_pairs={{0,2},{2,0},{1,3},{3,1},{4,6},{6,4},{5,7},{7,5},{8,10},{10,8},{9,1... | collective-permute-start | bytes 835592 | tf_op jit(solution)/shard_map/ppermute | solution.py:249
  27.0 10.2 %collective-permute-start.9 = (bf16[64,2176]{1,0:T(8,128)(2,1)S(1)}, bf16[64,2176]{1,0:T(8,128)(2,1)S(1)}, u32[]{:S(2)}, u32[]{:S(2)}) collective-permute-start(bf16[64,2176]{1,0:T(8,128)(2,1)S(1)} %collective-permute-done.6.refs_2_), channel_id=1, source_target_pairs={{0,1},{1,0},{2,3},{3,2},{4,5},{5,4},{6,7},{7,6},{8,9},{9,8},{10,11... | collective-permute-start | bytes 835592 | tf_op jit(solution)/shard_map/ppermute | solution.py:244
  34.8 2.4 %collective-permute-start.10 = (bf16[64,2176]{1,0:T(8,128)(2,1)S(1)}, bf16[64,2176]{1,0:T(8,128)(2,1)S(1)}, u32[]{:S(2)}, u32[]{:S(2)}) collective-permute-start(bf16[64,2176]{1,0:T(8,128)(2,1)S(1)} %shard_map.67.refs_3_), channel_id=1, source_target_pairs={{0,1},{1,0},{2,3},{3,2},{4,5},{5,4},{6,7},{7,6},{8,9},{9,8},{10,11... | collective-permute-start | bytes 835592 | tf_op jit(solution)/shard_map/ppermute | solution.py:244
  35.3 8.8 %collective-permute-start.12 = (bf16[64,2176]{1,0:T(8,128)(2,1)S(1)}, bf16[64,2176]{1,0:T(8,128)(2,1)S(1)}, u32[]{:S(2)}, u32[]{:S(2)}) collective-permute-start(bf16[64,2176]{1,0:T(8,128)(2,1)S(1)} %collective-permute-done.4.refs_0_.refs_1_), channel_id=1, source_target_pairs={{0,2},{2,0},{1,3},{3,1},{4,6},{6,4},{5,7},{7,5},{8,10},{10,8},{9,1... | collective-permute-start | bytes 835592 | tf_op jit(solution)/shard_map/ppermute | solution.py:249
  40.6 3.5 %collective-permute-start.11 = (bf16[2,64,2048]{2,1,0:T(8,128)(2,1)S(1)}, bf16[2,64,2048]{2,1,0:T(8,128)(2,1)S(1)}, u32[]{:S(2)}, u32[]{:S(2)}) collective-permute-start(bf16[2,64,2048]{2,1,0:T(8,128)(2,1)S(1)} %get-tuple-element.20), channel_id=1, source_target_pairs={{0,1},{1,0},{2,3},{3,2},{4,5},{5,4},{6,7},{7,6},{8,9},{9,8},{10,11... | collective-permute-start | bytes 1572872 | tf_op jit(solution)/shard_map/ppermute | solution.py:252
  40.6 5.3 %collective-permute-start.13 = (bf16[64,2176]{1,0:T(8,128)(2,1)S(1)}, bf16[64,2176]{1,0:T(8,128)(2,1)S(1)}, u32[]{:S(2)}, u32[]{:S(2)}) collective-permute-start(bf16[64,2176]{1,0:T(8,128)(2,1)S(1)} %collective-permute-done.4.refs_0_.refs_1_), channel_id=1, source_target_pairs={{0,1},{1,0},{2,3},{3,2},{4,5},{5,4},{6,7},{7,6},{8,9},{9,8},{10,11... | collective-permute-start | bytes 835592 | tf_op jit(solution)/shard_map/ppermute | solution.py:244
  41.1 4.8 %collective-permute-start.15 = (bf16[64,2176]{1,0:T(8,128)(2,1)S(1)}, bf16[64,2176]{1,0:T(8,128)(2,1)S(1)}, u32[]{:S(2)}, u32[]{:S(2)}) collective-permute-start(bf16[64,2176]{1,0:T(8,128)(2,1)S(1)} %collective-permute-done.5.refs_1_.refs_3_), channel_id=1, source_target_pairs={{0,1},{1,0},{2,3},{3,2},{4,5},{5,4},{6,7},{7,6},{8,9},{9,8},{10,11... | collective-permute-start | bytes 835592 | tf_op jit(solution)/shard_map/ppermute | solution.py:244
  41.2 4.7 %collective-permute-start.16 = (bf16[64,2176]{1,0:T(8,128)(2,1)S(1)}, bf16[64,2176]{1,0:T(8,128)(2,1)S(1)}, u32[]{:S(2)}, u32[]{:S(2)}) collective-permute-start(bf16[64,2176]{1,0:T(8,128)(2,1)S(1)} %collective-permute-done.8.refs_2_.refs_4_), channel_id=1, source_target_pairs={{0,1},{1,0},{2,3},{3,2},{4,5},{5,4},{6,7},{7,6},{8,9},{9,8},{10,11... | collective-permute-start | bytes 835592 | tf_op jit(solution)/shard_map/ppermute | solution.py:244
  44.2 8.8 %collective-permute-start.17 = (bf16[64,2048]{1,0:T(8,128)(2,1)S(1)}, bf16[64,2048]{1,0:T(8,128)(2,1)S(1)}, u32[]{:S(2)}, u32[]{:S(2)}) collective-permute-start(bf16[64,2048]{1,0:T(8,128)(2,1)S(1)} %shard_map.69.refs_0_), channel_id=1, source_target_pairs={{0,2},{2,0},{1,3},{3,1},{4,6},{6,4},{5,7},{7,5},{8,10},{10,8},{9,1... | collective-permute-start | bytes 786440 | tf_op jit(solution)/shard_map/ppermute | solution.py:254
  53.0 2.7 %collective-permute-start.18 = (bf16[2,128,2048]{2,1,0:T(8,128)(2,1)S(1)}, bf16[2,128,2048]{2,1,0:T(8,128)(2,1)S(1)}, u32[]{:S(2)}, u32[]{:S(2)}) collective-permute-start(bf16[2,128,2048]{2,1,0:T(8,128)(2,1)S(1)} %shard_map.72), channel_id=1, source_target_pairs={{0,1},{1,0},{2,3},{3,2},{4,5},{5,4},{6,7},{7,6},{8,9},{9,8},{10,11... | collective-permute-start | bytes 3145736 | tf_op jit(solution)/shard_map/ppermute | solution.py:256
  53.1 4.9 %collective-permute-start.3 = (bf16[2,64,2048]{2,1,0:T(8,128)(2,1)S(1)}, bf16[2,64,2048]{2,1,0:T(8,128)(2,1)S(1)}, u32[]{:S(2)}, u32[]{:S(2)}) collective-permute-start(bf16[2,64,2048]{2,1,0:T(8,128)(2,1)S(1)} %get-tuple-element.15.refs_1_), channel_id=1, source_target_pairs={{0,1},{1,0},{2,3},{3,2},{4,5},{5,4},{6,7},{7,6},{8,9},{9,8},{10,11... | collective-permute-start | bytes 1572872 | tf_op jit(solution)/shard_map/ppermute | solution.py:248
  53.6 8.3 %collective-permute-start.21 = (bf16[64,2048]{1,0:T(8,128)(2,1)S(1)}, bf16[64,2048]{1,0:T(8,128)(2,1)S(1)}, u32[]{:S(2)}, u32[]{:S(2)}) collective-permute-start(bf16[64,2048]{1,0:T(8,128)(2,1)S(1)} %shard_map.71.refs_1_), channel_id=1, source_target_pairs={{0,4},{4,0},{8,12},{12,8},{1,5},{5,1},{9,13},{13,9},{2,6},{6,2},{1... | collective-permute-start | bytes 786440 | tf_op jit(solution)/shard_map/ppermute | solution.py:257
  55.8 9.2 %collective-permute-start.20 = (bf16[64,2048]{1,0:T(8,128)(2,1)S(1)}, bf16[64,2048]{1,0:T(8,128)(2,1)S(1)}, u32[]{:S(2)}, u32[]{:S(2)}) collective-permute-start(bf16[64,2048]{1,0:T(8,128)(2,1)S(1)} %shard_map.73.refs_1_), channel_id=1, source_target_pairs={{0,2},{2,0},{1,3},{3,1},{4,6},{6,4},{5,7},{7,5},{8,10},{10,8},{9,1... | collective-permute-start | bytes 786440 | tf_op jit(solution)/shard_map/ppermute | solution.py:259
  57.7 13.0 %collective-permute-start.23 = (bf16[64,2048]{1,0:T(8,128)(2,1)S(1)}, bf16[64,2048]{1,0:T(8,128)(2,1)S(1)}, u32[]{:S(2)}, u32[]{:S(2)}) collective-permute-start(bf16[64,2048]{1,0:T(8,128)(2,1)S(1)} %shard_map.74.refs_2_), channel_id=1, source_target_pairs={{0,2},{2,0},{1,3},{3,1},{4,6},{6,4},{5,7},{7,5},{8,10},{10,8},{9,1... | collective-permute-start | bytes 786440 | tf_op jit(solution)/shard_map/ppermute | solution.py:259
  58.1 17.4 %collective-permute-start.19 = (bf16[64,2048]{1,0:T(8,128)(2,1)S(1)}, bf16[64,2048]{1,0:T(8,128)(2,1)S(1)}, u32[]{:S(2)}, u32[]{:S(2)}) collective-permute-start(bf16[64,2048]{1,0:T(8,128)(2,1)S(1)} %shard_map.75), channel_id=1, source_target_pairs={{0,2},{2,0},{1,3},{3,1},{4,6},{6,4},{5,7},{7,5},{8,10},{10,8},{9,1... | collective-permute-start | bytes 786440 | tf_op jit(solution)/shard_map/ppermute | solution.py:260
  65.2 10.3 %collective-permute-start.22 = (bf16[64,2048]{1,0:T(8,128)(2,1)S(1)}, bf16[64,2048]{1,0:T(8,128)(2,1)S(1)}, u32[]{:S(2)}, u32[]{:S(2)}) collective-permute-start(bf16[64,2048]{1,0:T(8,128)(2,1)S(1)} %shard_map.76), channel_id=1, source_target_pairs={{0,12},{4,8},{8,4},{12,0},{1,13},{5,9},{9,5},{13,1},{2,14},{6,10},... | collective-permute-start | bytes 786440 | tf_op jit(solution)/shard_map/ppermute | solution.py:262
  70.7 8.7 %collective-permute-start.24 = (bf16[64,2048]{1,0:T(8,128)(2,1)S(1)}, bf16[64,2048]{1,0:T(8,128)(2,1)S(1)}, u32[]{:S(2)}, u32[]{:S(2)}) collective-permute-start(bf16[64,2048]{1,0:T(8,128)(2,1)S(1)} %shard_map.77), channel_id=1, source_target_pairs={{0,4},{4,0},{8,12},{12,8},{1,5},{5,1},{9,13},{13,9},{2,6},{6,2},{1... | collective-permute-start | bytes 786440 | tf_op jit(solution)/shard_map/ppermute | solution.py:263
  (1 other events, 1.9 us)
